TPU v7x, 32 devices: a whole 2x2x4 slice. The times are simulated.
32 devices in a mesh: img: 8 (over y, x, core), seq: 4 (over z).
Axes of the slice: x: 2, y: 2, z: 4, core: 2. Of those that a mesh axis runs over, the one named last changes fastest.
Arguments:
- tokens: bfloat16 [24, 1376, 1024], P('img', 'seq'), may hold values from -6 to 6
- cotangent: bfloat16 [24, 1376, 1024], P('img', 'seq'), may hold values from -6 to 6
- token_mask: int32 [24, 1376], P('img'), may hold values from 0 to 1, as said below
- slot_flags: int32 [24], P('img'), may hold values 0 or 1
- w_qkv: bfloat16 [1024, 3072], P('img'), may hold values from -0.1875 to 0.1875
- w_out: bfloat16 [1024, 1024], P('img'), may hold values from -3 to 3
- w_up: bfloat16 [1024, 4096], P('img'), may hold values from -0.1875 to 0.1875
- w_down: bfloat16 [4096, 1024], P('img'), may hold values from -0.09375 to 0.09375
- norm_gain: bfloat16 [2, 1024], P(None, 'img'), may hold values from 0.5 to 1.5
- norm_bias: bfloat16 [2, 1024], P(None, 'img'), may hold values from -1.796875 to 1.796875
- proj_bias: bfloat16 [4, 1024], P(None, 'img'), may hold values from -1.796875 to 1.796875
- up_bias: bfloat16 [4096], P('img'), may hold values from -1.796875 to 1.796875
- layer_scale: bfloat16 [2, 1024], P(None, 'img'), may hold values from 0.5 to 1.5
Outputs:
- output: bfloat16 [24, 1376, 1024], P('img', 'seq')
- grad_tokens: bfloat16 [24, 1376, 1024], P('img', 'seq')
- grad_w_qkv: float32 [1024, 3072], P('img')
- grad_w_out: float32 [1024, 1024], P('img')
- grad_w_up: float32 [1024, 4096], P('img')
- grad_w_down: float32 [4096, 1024], P('img')
- grad_norm_gain: float32 [2, 1024], P(None, 'img')
- grad_norm_bias: float32 [2, 1024], P(None, 'img')
- grad_proj_bias: float32 [4, 1024], P(None, 'img')
- grad_up_bias: float32 [4096], P('img')
- grad_layer_scale: float32 [2, 1024], P(None, 'img')
Inputs may be any that keep to these rules, and one draw needn't show every extreme that they name: `token_mask`: each slot's real tokens are its first positions, at least 688 of them; some slot is full in every draw.
All inputs are finite; a program needn't handle non-finite values. No bound on the sum of `slot_flags` on one device may be relied on, other than what follows from the above.
Results may differ from a plain program's by a relative error of at most 0.018.
Values may be sent and summed in bfloat16 or wider, within the bound.
A program may use at most 320 MiB of HBM per device.

v0:
```python
import jax
import jax.numpy as jnp
from jax import lax
from jax.experimental import pallas as pl
from jax.experimental.pallas import tpu as pltpu
from jax.sharding import PartitionSpec as P

HD = 64
PAIR = 2 * HD


norm_eps = 1e-06


def norm_rows(values, gain, shift):
    center = values - jnp.mean(values, axis=-1, keepdims=True)
    spread = jnp.mean(center * center, axis=-1, keepdims=True)
    return center * lax.rsqrt(spread + norm_eps) * gain + shift


def gelu_and_slope(values):
    half = 0.5 + 0.5 * lax.erf(values * 0.5**0.5)
    slope = half + values * jnp.exp(-0.5 * values * values) * (0.5 / jnp.pi) ** 0.5
    return (values * half).astype(jnp.bfloat16), slope


def chunks_of(total):
    cuts = list(range(0, total, 512)) + [total]
    return [(cuts[n], cuts[n + 1] - cuts[n]) for n in range(len(cuts) - 1)]


def lane_of(rows):
    return lax.broadcasted_iota(jnp.int32, (rows, PAIR), 1)


def in_three(values):
    high = values.astype(jnp.bfloat16).astype(jnp.float32)
    rest = values - high
    mid = rest.astype(jnp.bfloat16).astype(jnp.float32)
    return high, mid, rest - mid


def dot_nt(left, right):
    return lax.dot_general(left, right, (((1,), (1,)), ((), ())), preferred_element_type=jnp.float32)


def attend_kernel(qkv_ref, bias_ref, out_ref, log_ref):
    seq_len, width = out_ref.shape
    lane = lane_of(seq_len)
    bias = jnp.broadcast_to(bias_ref[...], (seq_len, PAIR))
    ones = jnp.ones((seq_len, PAIR), jnp.bfloat16)
    key_extra = jnp.where(lane == 0, bias, 0.0).astype(jnp.bfloat16)
    for pair in range(width // PAIR):
        at = pair * PAIR
        keys = qkv_ref[:, width + at : width + at + PAIR]
        values = qkv_ref[:, 2 * width + at : 2 * width + at + PAIR]
        value_wide = jnp.concatenate([values, ones], axis=1)
        for start, size in chunks_of(seq_len):
            rows = slice(start, start + size)
            first = lane_of(size) < HD
            query = qkv_ref[rows, at : at + PAIR] * jnp.bfloat16(0.125)
            query_extra = jnp.where(lane_of(size) == 0, 1.0, 0.0).astype(jnp.bfloat16)
            query_wide = jnp.concatenate([query, query_extra], axis=1)
            parts = []
            for half in range(2):
                own = (lane >= HD) if half else (lane < HD)
                key_own = jnp.where(own, keys.astype(jnp.float32), 0.0).astype(jnp.bfloat16)
                key_wide = jnp.concatenate([key_own, key_extra], axis=1)
                scores = dot_nt(query_wide, key_wide)
                row_max = jnp.max(scores, axis=1, keepdims=True)
                weights = jnp.exp(scores - row_max).astype(jnp.bfloat16)
                mixed = jnp.dot(weights, value_wide, preferred_element_type=jnp.float32)
                total = mixed[:, PAIR:]
                parts.append((mixed[:, :PAIR] / total, row_max + jnp.log(total)))
            out_ref[rows, at : at + PAIR] = jnp.where(first, parts[0][0], parts[1][0]).astype(
                out_ref.dtype
            )
            log_ref[rows, at : at + PAIR] = jnp.where(first, parts[0][1], parts[1][1])


def attend_back_kernel(qkv_ref, bias_ref, log_ref, out_ref, grad_ref, dqkv_ref):
    seq_len, width = out_ref.shape
    lane = lane_of(seq_len)
    place = lax.rem(lane, HD)
    bias = jnp.broadcast_to(bias_ref[...], (seq_len, PAIR))
    minus = jnp.where(place < 3, -1.0, 0.0)
    key_tail = jnp.where(place == 3, bias, minus)
    for pair in range(width // PAIR):
        at = pair * PAIR
        query = qkv_ref[:, at : at + PAIR] * jnp.bfloat16(0.125)
        keys = qkv_ref[:, width + at : width + at + PAIR].astype(jnp.float32)
        values = qkv_ref[:, 2 * width + at : 2 * width + at + PAIR].astype(jnp.float32)
        grad = grad_ref[:, at : at + PAIR]
        high, mid, low = in_three(log_ref[:, at : at + PAIR])
        tail = jnp.where(place == 0, high, jnp.where(place == 1, mid, low))
        tail = jnp.where(place < 3, tail, jnp.where(place == 3, 1.0, 0.0))
        query_wide = jnp.concatenate([query, tail.astype(jnp.bfloat16)], axis=1)
        product = grad.astype(jnp.float32) * out_ref[:, at : at + PAIR].astype(jnp.float32)
        inner_a = jnp.sum(jnp.where(lane < HD, product, 0.0), axis=1, keepdims=True)
        inner_b = jnp.sum(jnp.where(lane < HD, 0.0, product), axis=1, keepdims=True)
        high, mid, low = in_three(jnp.where(lane < HD, inner_a, inner_b))
        tail = jnp.where(place == 0, high, jnp.where(place == 1, mid, low))
        tail = jnp.where(place < 3, tail, 0.0)
        grad_wide = jnp.concatenate([grad, tail.astype(jnp.bfloat16)], axis=1)
        total_q = [None, None]
        for start, size in chunks_of(seq_len):
            rows = slice(start, start + size)
            first = lane_of(size) < HD
            keys_here = keys[rows].astype(jnp.bfloat16)
            parts = []
            for half in range(2):
                own = jnp.logical_not(first) if half else first
                key_wide = jnp.concatenate(
                    [jnp.where(own, keys[rows], 0.0), jnp.where(own, key_tail[rows], 0.0)], axis=1
                ).astype(jnp.bfloat16)
                value_wide = jnp.concatenate(
                    [jnp.where(own, values[rows], 0.0), jnp.where(own, minus[rows], 0.0)], axis=1
                ).astype(jnp.bfloat16)
                probs = jnp.exp(dot_nt(key_wide, query_wide))
                grad_scores = (probs * dot_nt(value_wide, grad_wide)).astype(jnp.bfloat16)
                grad_value = jnp.dot(
                    probs.astype(jnp.bfloat16), grad, preferred_element_type=jnp.float32
                )
                grad_key = jnp.dot(grad_scores, query, preferred_element_type=jnp.float32)
                part_q = lax.dot_general(
                    grad_scores,
                    keys_here,
                    (((0,), (0,)), ((), ())),
                    preferred_element_type=jnp.float32,
                )
                total_q[half] = part_q if total_q[half] is None else total_q[half] + part_q
                parts.append((grad_key, grad_value))
            dqkv_ref[rows, width + at : width + at + PAIR] = jnp.where(
                first, parts[0][0], parts[1][0]
            ).astype(dqkv_ref.dtype)
            dqkv_ref[rows, 2 * width + at : 2 * width + at + PAIR] = jnp.where(
                first, parts[0][1], parts[1][1]
            ).astype(dqkv_ref.dtype)
        dqkv_ref[:, at : at + PAIR] = (jnp.where(lane < HD, total_q[0], total_q[1]) * 0.125).astype(
            dqkv_ref.dtype
        )


def attend(qkv, key_bias):
    seq_len, triple = qkv.shape
    width = triple // 3
    return pl.pallas_call(
        attend_kernel,
        out_shape=(
            jax.ShapeDtypeStruct((seq_len, width), jnp.bfloat16),
            jax.ShapeDtypeStruct((seq_len, width), jnp.float32),
        ),
        cost_estimate=pl.CostEstimate(
            flops=16 * seq_len * seq_len * width,
            bytes_accessed=14 * seq_len * width,
            transcendentals=seq_len * seq_len * width // HD,
        ),
        compiler_params=pltpu.CompilerParams(vmem_limit_bytes=48 * 1024 * 1024),
        name="attend",
    )(qkv, key_bias)


def attend_back(qkv, key_bias, log_total, mixed, grad_mixed):
    seq_len, triple = qkv.shape
    width = triple // 3
    return pl.pallas_call(
        attend_back_kernel,
        out_shape=jax.ShapeDtypeStruct((seq_len, triple), jnp.bfloat16),
        cost_estimate=pl.CostEstimate(
            flops=40 * seq_len * seq_len * width,
            bytes_accessed=20 * seq_len * width,
            transcendentals=seq_len * seq_len * width // HD,
        ),
        compiler_params=pltpu.CompilerParams(vmem_limit_bytes=48 * 1024 * 1024),
        name="attend_back",
    )(qkv, key_bias, log_total, mixed, grad_mixed)


def body(
    tokens,
    cotangent,
    token_mask,
    slot_flags,
    w_qkv,
    w_out,
    w_up,
    w_down,
    norm_gain,
    norm_bias,
    proj_bias,
    up_bias,
    layer_scale,
):
    seq_count = lax.axis_size("seq")
    seq_place = lax.axis_index("seq")
    img_count = lax.axis_size("img")
    img_place = lax.axis_index("img")
    images, local_rows, model_width = tokens.shape
    seq_len = token_mask.shape[1]
    head_cols = model_width // seq_count
    group = 3 * head_cols
    shard = norm_gain.shape[1]
    up_rows = up_bias.shape[0] // shard
    row_mask = lax.dynamic_slice_in_dim(token_mask, seq_place * local_rows, local_rows, 1)
    live_rows = (row_mask * slot_flags[:, None]).astype(jnp.float32).reshape(-1, 1)
    key_bias = jnp.where(token_mask > 0, 0.0, -1e30).astype(jnp.float32)

    def by_group(matrix):
        rows = matrix.shape[0]
        return matrix.reshape(rows, 3, seq_count, head_cols).swapaxes(1, 2).reshape(rows, -1)

    def by_kind(matrix):
        rows = matrix.shape[0]
        return matrix.reshape(rows, seq_count, 3, head_cols).swapaxes(1, 2).reshape(rows, -1)

    small = jnp.concatenate(
        [norm_gain, norm_bias, proj_bias, layer_scale, up_bias.reshape(up_rows, shard)], axis=0
    )
    small = lax.all_gather(small, "img", axis=0, tiled=False).astype(jnp.float32)
    up_bias_f = small[:, 10:].reshape(-1)
    small = small.swapaxes(0, 1).reshape(-1, model_width)
    gain_f, shift_f, bias_f, scale_f = (small[0:2], small[2:4], small[4:8], small[8:10])
    qkv_full = lax.all_gather(by_group(w_qkv), "img", axis=0, tiled=True)
    out_full = lax.all_gather(w_out, "img", axis=0, tiled=True)
    up_full = lax.all_gather(w_up, "img", axis=0, tiled=True)
    down_full = lax.all_gather(w_down, "img", axis=0, tiled=True)

    inputs = tokens.reshape(-1, model_width).astype(jnp.float32)
    normed_one, norm_one_pull = jax.vjp(norm_rows, inputs, gain_f[0], shift_f[0])
    normed_one = normed_one.astype(jnp.bfloat16)
    shift_qkv = jnp.concatenate([bias_f[0], jnp.zeros((model_width,), jnp.float32), bias_f[1]])
    shift_qkv = by_group(shift_qkv[None])
    normed_by_image = normed_one.reshape(images, local_rows, model_width)
    saved = []
    returned = []
    for slot in range(images):
        qkv = jnp.dot(normed_by_image[slot], qkv_full, preferred_element_type=jnp.float32)
        qkv = (qkv + shift_qkv).astype(jnp.bfloat16)
        qkv = jnp.stack([qkv[:, n * group : (n + 1) * group] for n in range(seq_count)])
        spread = lax.all_to_all(qkv, "seq", split_axis=0, concat_axis=0, tiled=True)
        spread = spread.reshape(seq_len, group)
        slot_bias = key_bias[slot][:, None]
        mixed, log_total = attend(spread, slot_bias)
        saved.append((spread, slot_bias, log_total, mixed))
        back = lax.all_to_all(
            mixed.reshape(seq_count, local_rows, head_cols),
            "seq",
            split_axis=0,
            concat_axis=0,
            tiled=True,
        )
        returned.append(jnp.concatenate([back[n] for n in range(seq_count)], axis=1))
    attended = jnp.stack(returned).reshape(-1, model_width)
    branch = jnp.dot(attended, out_full, preferred_element_type=jnp.float32) + bias_f[2]
    middle = inputs + scale_f[0] * branch
    normed_two, norm_two_pull = jax.vjp(norm_rows, middle, gain_f[1], shift_f[1])
    normed_two = normed_two.astype(jnp.bfloat16)
    up_proj = jnp.dot(normed_two, up_full, preferred_element_type=jnp.float32) + up_bias_f
    activated, gelu_slope = lax.optimization_barrier(gelu_and_slope(up_proj))
    down_proj = jnp.dot(activated, down_full, preferred_element_type=jnp.float32) + bias_f[3]
    result = (
        ((middle + scale_f[1] * down_proj) * live_rows).astype(jnp.bfloat16).reshape(tokens.shape)
    )
    grad_y = cotangent.reshape(-1, model_width).astype(jnp.float32) * live_rows
    grad_scale_two = jnp.sum(grad_y * down_proj, axis=0)
    grad_down = (grad_y * scale_f[1]).astype(jnp.bfloat16)
    grad_bias_down = jnp.sum(grad_down.astype(jnp.float32), axis=0)
    grad_act = jnp.dot(grad_down, down_full.T, preferred_element_type=jnp.float32)
    grad_up = (grad_act * gelu_slope).astype(jnp.bfloat16)
    grad_up_bias = jnp.sum(grad_up.astype(jnp.float32), axis=0)
    grad_normed_two = jnp.dot(grad_up, up_full.T, preferred_element_type=jnp.float32)
    grad_from_two, grad_gain_two, grad_shift_two = norm_two_pull(grad_normed_two)
    grad_middle = grad_y + grad_from_two
    grad_scale_one = jnp.sum(grad_middle * branch, axis=0)
    grad_branch = (grad_middle * scale_f[0]).astype(jnp.bfloat16)
    grad_bias_out = jnp.sum(grad_branch.astype(jnp.float32), axis=0)
    grad_attended = jnp.dot(grad_branch, out_full.T, preferred_element_type=jnp.float32).astype(
        jnp.bfloat16
    )
    grad_attended = grad_attended.reshape(images, local_rows, model_width)

    def owned(left, right):
        grad = jnp.dot(left.T, right, preferred_element_type=jnp.float32).astype(jnp.bfloat16)
        return lax.psum_scatter(grad, "img", scatter_dimension=0, tiled=True)

    grad_w_down = owned(activated, grad_down)
    grad_w_up = owned(normed_two, grad_up)
    grad_w_out = owned(attended, grad_branch)
    grad_parts = []
    for slot in range(images):
        grad_here = grad_attended[slot]
        grad_here = jnp.stack(
            [grad_here[:, n * head_cols : (n + 1) * head_cols] for n in range(seq_count)]
        )
        grad_mixed = lax.all_to_all(grad_here, "seq", split_axis=0, concat_axis=0, tiled=True)
        if slot == images - 1:
            grad_mixed, grad_w_down, grad_w_up, grad_w_out = lax.optimization_barrier(
                (grad_mixed, grad_w_down, grad_w_up, grad_w_out)
            )
            grad_w_down, grad_w_up, grad_w_out = lax.psum(
                (grad_w_down, grad_w_up, grad_w_out), "seq"
            )
        spread, slot_bias, log_total, mixed = saved[slot]
        grad_spread = attend_back(
            spread, slot_bias, log_total, mixed, grad_mixed.reshape(seq_len, head_cols)
        )
        back = lax.all_to_all(
            grad_spread.reshape(seq_count, local_rows, group),
            "seq",
            split_axis=0,
            concat_axis=0,
            tiled=True,
        )
        grad_parts.append(jnp.concatenate([back[n] for n in range(seq_count)], axis=1))
    grad_qkv = jnp.stack(grad_parts).reshape(-1, 3 * model_width)
    grad_qkv, grad_w_down, grad_w_up, grad_w_out = lax.optimization_barrier(
        (grad_qkv, grad_w_down, grad_w_up, grad_w_out)
    )
    grad_w_qkv = owned(normed_one, grad_qkv)
    grad_bias_qkv = by_kind(jnp.sum(grad_qkv.astype(jnp.float32), axis=0)[None])[0]
    grad_normed_one = jnp.dot(grad_qkv, qkv_full.T, preferred_element_type=jnp.float32)
    grad_from_one, grad_gain_one, grad_shift_one = norm_one_pull(grad_normed_one)
    grad_inputs = (grad_middle + grad_from_one).astype(jnp.bfloat16).reshape(tokens.shape)
    grad_w_qkv = by_kind(lax.psum(grad_w_qkv, "seq"))
    smalls = jnp.stack(
        [
            grad_gain_one,
            grad_gain_two,
            grad_shift_one,
            grad_shift_two,
            grad_bias_qkv[:model_width],
            grad_bias_qkv[2 * model_width :],
            grad_bias_out,
            grad_bias_down,
            grad_scale_one,
            grad_scale_two,
        ]
    )
    grad_up_bias = grad_up_bias.reshape(img_count, up_rows, shard).swapaxes(0, 1)
    smalls = jnp.concatenate([smalls, grad_up_bias.reshape(up_rows, model_width)], axis=0)
    smalls = lax.psum(smalls, ("img", "seq"))
    smalls = lax.dynamic_slice_in_dim(smalls, img_place * shard, shard, 1)
    return (
        result,
        grad_inputs,
        grad_w_qkv.astype(jnp.float32),
        grad_w_out.astype(jnp.float32),
        grad_w_up.astype(jnp.float32),
        grad_w_down.astype(jnp.float32),
        smalls[0:2],
        smalls[2:4],
        smalls[4:8],
        smalls[10:].reshape(-1),
        smalls[8:10],
    )


def solution(mesh):
    placed = (
        P("img", "seq", None),
        P("img", "seq", None),
        P("img", None),
        P("img"),
        P("img", None),
        P("img", None),
        P("img", None),
        P("img", None),
        P(None, "img"),
        P(None, "img"),
        P(None, "img"),
        P("img"),
        P(None, "img"),
    )
    return jax.shard_map(
        body,
        mesh=mesh,
        in_specs=placed,
        out_specs=(
            P("img", "seq", None),
            P("img", "seq", None),
            P("img", None),
            P("img", None),
            P("img", None),
            P("img", None),
            P(None, "img"),
            P(None, "img"),
            P(None, "img"),
            P("img"),
            P(None, "img"),
        ),
        check_vma=False,
    )
```

profile of v0, /device:TPU:0, one launch (start us, length us, event | category | flops | bytes accessed | tf_op | source)
XLA Modules:
  0.0 873.0 jit_solution(6926558797786615224)
XLA Ops:
  13.3 10.5 %all-gather.1 = bf16[8,14,128]{2,1,0:T(8,128)(2,1)S(1)} all-gather(bf16[1,14,128]{2,1,0:T(8,128)(2,1)S(1)} %bitcast.248), channel_id=2, replica_groups=mesh['img'=8,'seq'=4] {'img'}, dimensions={0}, use_global_device_ids=true | all-gather | bytes 32256 | tf_op jit(solution)/shard_map/all_gather | solution.py:219
  26.6 33.2 %all-gather.7.cloned.1.call-done = bf16[1024,3072]{0,1:T(8,128)(2,1)} async-done(((bf16[128,3072]{0,1:T(8,128)(2,1)}), bf16[1024,3072]{0,1:T(8,128)(2,1)}) %all-gather.7.cloned.1.call-update) | async-done | bytes 6291472 | tf_op jit(solution)/shard_map/all_gather | solution.py:223
  59.9 5.4 add_convert_fusion.2
  67.1 4.6 all-to-all-start.4
  72.2 5.4 add_convert_fusion.4
  79.4 41.2 %all-to-all-done.4 = bf16[4,344,768]{2,1,0:T(8,128)(2,1)S(1)} async-done(((bf16[4,344,768]{2,1,0:T(8,128)(2,1)}), bf16[4,344,768]{2,1,0:T(8,128)(2,1)S(1)}, u32[]{:S(2)}, u32[]{:S(2)}) %all-to-all-start.4) | async-done | bytes 2113568 | tf_op jit(solution)/shard_map/all_to_all | solution.py:240
  120.6 4.4 all-to-all-start
  125.1 5.4 add_convert_fusion.3
  132.3 41.0 %all-to-all-done = bf16[4,344,768]{2,1,0:T(8,128)(2,1)} async-done(((bf16[4,344,768]{2,1,0:T(8,128)(2,1)}), bf16[4,344,768]{2,1,0:T(8,128)(2,1)}, u32[]{:S(2)}, u32[]{:S(2)}) %all-to-all-start) | async-done | bytes 2113568 | tf_op jit(solution)/shard_map/all_to_all | solution.py:240
  173.3 4.8 all-to-all-start.2
  179.0 13.3 %attend.3 = (bf16[1376,256]{1,0:T(8,128)(2,1)}, f32[1376,256]{1,0:T(8,128)S(1)}) custom-call(bf16[1376,768]{1,0:T(8,128)(2,1)} %bitcast.17.qkv_ref, f32[1376,1]{1,0:T(8,128)S(1)} %copy.47.bias_ref), custom_call_target="tpu_custom_call" | custom-call | flops 7755268096 | bytes 4931584 | tf_op jit(solution)/shard_map/attend/pallas_call | solution.py:147
  193.5 32.5 %all-to-all-done.2 = bf16[4,344,768]{2,1,0:T(8,128)(2,1)} async-done(((bf16[4,344,768]{2,1,0:T(8,128)(2,1)}), bf16[4,344,768]{2,1,0:T(8,128)(2,1)}, u32[]{:S(2)}, u32[]{:S(2)}) %all-to-all-start.2) | async-done | bytes 2113568 | tf_op jit(solution)/shard_map/all_to_all | solution.py:240
  226.0 4.0 all-to-all-start.1
  231.0 11.5 %attend.5 = (bf16[1376,256]{1,0:T(8,128)(2,1)}, f32[1376,256]{1,0:T(8,128)S(1)}) custom-call(bf16[1376,768]{1,0:T(8,128)(2,1)S(1)} %bitcast.216, f32[1376,1]{1,0:T(8,128)S(1)} %copy.49.bias_ref), custom_call_target="tpu_custom_call" | custom-call | flops 7755268096 | bytes 4931584 | tf_op jit(solution)/shard_map/attend/pallas_call | solution.py:147
  243.5 4.3 all-to-all-done.1
  247.8 4.4 all-to-all-start.5
  254.6 13.3 %attend.4 = (bf16[1376,256]{1,0:T(8,128)(2,1)}, f32[1376,256]{1,0:T(8,128)S(1)}) custom-call(bf16[1376,768]{1,0:T(8,128)(2,1)} %bitcast.29.qkv_ref, f32[1376,1]{1,0:T(8,128)S(1)} %copy.48.bias_ref), custom_call_target="tpu_custom_call" | custom-call | flops 7755268096 | bytes 4931584 | tf_op jit(solution)/shard_map/attend/pallas_call | solution.py:147
  270.1 4.2 all-to-all-start.3
  280.9 11.3 %all-to-all-done.3 = bf16[4,344,256]{2,1,0:T(8,128)(2,1)} async-done(((bf16[4,344,256]{2,1,0:T(8,128)(2,1)}), bf16[4,344,256]{2,1,0:T(8,128)(2,1)}, u32[]{:S(2)}, u32[]{:S(2)}) %all-to-all-start.3) | async-done | bytes 704544 | tf_op jit(solution)/shard_map/all_to_all | solution.py:245
  296.4 7.9 multiply_add_fusion.1
  309.7 22.9 %fusion.3 = (f32[1032,4096]{1,0:T(8,128)}, bf16[1032,4096]{1,0:T(8,128)(2,1)}) fusion(f32[4096]{0:T(1024)S(1)} %bitcast.249, bf16[1024,4096]{1,0:T(8,128)(2,1)} %all-gather.11.cloned.1.call-done, f32[1032,1024]{1,0:T(8,128)} %get-tuple-element.152, f32[1024]{0:T(1024)S(1)} %bitcast.258, f32[1024]{0:T(1024)S(1)} %bitcast.242, f32[1032]{0:T(1024)S(1)} %fusion.8, ...), kind=kOutput, calls=%fused_computation.6 | convolution fusion | flops 8708825088 | bytes 38010944 | tf_op jit(solution)/shard_map/dot_general | solution.py:258
  332.6 17.1 %convert_reduce_fusion = (f32[4096]{0:T(1024)}, bf16[1032,4096]{1,0:T(8,128)(2,1)}) fusion(f32[1032,4096]{1,0:T(8,128)} %get-tuple-element.31, bf16[1032,1024]{1,0:T(8,128)(2,1)S(1)} %copy-done.19, bf16[4096,1024]{1,0:T(8,128)(2,1)} %all-gather.13.cloned.1.call-done), kind=kOutput, calls=%fused_computation.7 | convolution fusion | flops 8673947648 | bytes 35880960 | tf_op jit(solution)/shard_map/dot_general | solution.py:268
  349.7 16.8 %multiply_reduce_fusion.2 = (f32[1024]{0:T(1024)}, f32[1032]{0:T(1024)S(1)}, f32[1024]{0:T(1024)}, f32[1032,1024]{1,0:T(8,128)S(1)}) fusion(f32[1032,1024]{1,0:T(8,128)} %get-tuple-element.152, f32[1032]{0:T(1024)S(1)} %fusion.8, f32[1032]{0:T(1024)S(1)} %broadcast_multiply_fusion, f32[1024]{0:T(1024)S(1)} %bitcast.243, ...), kind=kOutput, calls=%fused_computation.26 | convolution fusion | flops 8665494528 | bytes 25321568 | tf_op jit(solution)/shard_map/dot_general | solution.py:271
  366.5 3.6 fusion.9
  373.6 4.2 convolution_convert_fusion.4
  377.8 18.1 %convolution_convert_fusion.1 = bf16[1024,4096]{1,0:T(8,128)(2,1)} fusion(bf16[1032,4096]{1,0:T(8,128)(2,1)} %get-tuple-element.157, f32[1032,1024]{1,0:T(8,128)} %get-tuple-element.152, f32[1024]{0:T(1024)S(1)} %bitcast.259, f32[1024]{0:T(1024)S(1)} %bitcast.245, f32[1032]{0:T(1024)S(1)} %fusion.8, f32[1032]{0:T(1024)S(1)} %broadcast_multiply_fusion), kind=kOutput, calls=%fused_computation.13 | convolution fusion | flops 8666521600 | bytes 21086272 | tf_op jit(solution)/shard_map/dot_general | solution.py:283
  396.0 18.4 %convolution_convert_fusion = bf16[4096,1024]{1,0:T(8,128)(2,1)} fusion(bf16[1032,4096]{1,0:T(8,128)(2,1)} %get-tuple-element.30, bf16[1032,1024]{1,0:T(8,128)(2,1)S(1)} %copy-done.19), kind=kOutput, calls=%fused_computation.12 | convolution fusion | flops 8661237760 | bytes 18956288 | tf_op jit(solution)/shard_map/dot_general | solution.py:283
  416.0 4.0 convolution_convert_fusion.3
  425.6 16.7 %all-to-all-done.6 = bf16[4,344,256]{2,1,0:T(8,128)(2,1)S(1)} async-done(((bf16[4,344,256]{2,1,0:T(8,128)(2,1)}), bf16[4,344,256]{2,1,0:T(8,128)(2,1)S(1)}, u32[]{:S(2)}, u32[]{:S(2)}) %all-to-all-start.6) | async-done | bytes 704544 | tf_op jit(solution)/shard_map/all_to_all | solution.py:295
  446.7 16.9 %all-to-all-done.10 = bf16[4,344,256]{2,1,0:T(8,128)(2,1)S(1)} async-done(((bf16[4,344,256]{2,1,0:T(8,128)(2,1)}), bf16[4,344,256]{2,1,0:T(8,128)(2,1)S(1)}, u32[]{:S(2)}, u32[]{:S(2)}) %all-to-all-start.10) | async-done | bytes 704544 | tf_op jit(solution)/shard_map/all_to_all | solution.py:295
  463.6 3.9 all-to-all-start.8
  468.8 25.1 %attend_back.3 = bf16[1376,768]{1,0:T(8,128)(2,1)} custom-call(bf16[1376,768]{1,0:T(8,128)(2,1)} %bitcast.17.qkv_ref, f32[1376,1]{1,0:T(8,128)S(1)} %copy-done.2, f32[1376,256]{1,0:T(8,128)S(1)} %copy-done.8, bf16[1376,256]{1,0:T(8,128)(2,1)} %get-tuple-element.27.out_ref, bf16[1376,256]{1,0:T(8,128)(2,1)S(1)} %bitcast.219), custom_call_target="tpu_custom_call" | custom-call | flops 19388170240 | bytes 7045120 | tf_op jit(solution)/shard_map/attend_back/pallas_call | solution.py:166
  493.9 5.3 all-to-all-start.7
  500.6 25.7 %attend_back.4 = bf16[1376,768]{1,0:T(8,128)(2,1)} custom-call(bf16[1376,768]{1,0:T(8,128)(2,1)} %bitcast.29.qkv_ref, f32[1376,1]{1,0:T(8,128)S(1)} %copy-done.4, f32[1376,256]{1,0:T(8,128)S(1)} %copy-done.10, bf16[1376,256]{1,0:T(8,128)(2,1)} %get-tuple-element.28.out_ref, bf16[1376,256]{1,0:T(8,128)(2,1)S(1)} %bitcast.220), custom_call_target="tpu_custom_call" | custom-call | flops 19388170240 | bytes 7045120 | tf_op jit(solution)/shard_map/attend_back/pallas_call | solution.py:166
  526.3 20.3 %all-to-all-done.7 = bf16[4,344,768]{2,1,0:T(8,128)(2,1)} async-done(((bf16[4,344,768]{2,1,0:T(8,128)(2,1)}), bf16[4,344,768]{2,1,0:T(8,128)(2,1)}, u32[]{:S(2)}, u32[]{:S(2)}) %all-to-all-start.7) | async-done | bytes 2113568 | tf_op jit(solution)/shard_map/all_to_all | solution.py:307
  546.7 3.8 all-to-all-start.9
  550.5 16.7 %reduce-scatter.5.cloned.1.call-done = bf16[512,1024]{1,0:T(8,128)(2,1)} async-done(((bf16[4096,1024]{1,0:T(8,128)(2,1)}), bf16[512,1024]{1,0:T(8,128)(2,1)}) %reduce-scatter.5.cloned.1.call-update) | async-done | bytes 1048592 | tf_op jit(solution)/shard_map/reduce_scatter | solution.py:284
  568.6 25.2 %attend_back.5 = bf16[1376,768]{1,0:T(8,128)(2,1)} custom-call(bf16[1376,768]{1,0:T(8,128)(2,1)} %bitcast.217, f32[1376,1]{1,0:T(8,128)S(1)} %copy.49.bias_ref, f32[1376,256]{1,0:T(8,128)S(1)} %copy-done.6, bf16[1376,256]{1,0:T(8,128)(2,1)} %get-tuple-element.29.out_ref, bf16[1376,256]{1,0:T(8,128)(2,1)S(1)} %bitcast.218), custom_call_target="tpu_custom_call" | custom-call | flops 19388170240 | bytes 7045120 | tf_op jit(solution)/shard_map/attend_back/pallas_call | solution.py:166
  593.8 4.5 all-to-all-done.9
  598.3 4.4 all-to-all-start.11
  607.2 81.8 %all-to-all-done.11 = bf16[4,344,768]{2,1,0:T(8,128)(2,1)} async-done(((bf16[4,344,768]{2,1,0:T(8,128)(2,1)}), bf16[4,344,768]{2,1,0:T(8,128)(2,1)}, u32[]{:S(2)}, u32[]{:S(2)}) %all-to-all-start.11) | async-done | bytes 2113568 | tf_op jit(solution)/shard_map/all_to_all | solution.py:307
  694.5 42.7 %all-reduce.6.cloned.1.call-done = (bf16[512,1024]{1,0:T(8,128)(2,1)}, bf16[128,4096]{1,0:T(8,128)(2,1)}, bf16[128,1024]{1,0:T(8,128)(2,1)}) async-done(((bf16[512,1024]{1,0:T(8,128)(2,1)}, bf16[128,4096]{1,0:T(8,128)(2,1)}, bf16[128,1024]{1,0:T(8,128)(2,1)}), (bf16[512,1024]{1,0:T(8,128)(2,1)}, bf16[128,4096]{1,0:T(8,128)(2,1)}, bf16[128,1024]{1,0:T(8,128)(2,1)})) %all-reduce.6.cloned.1.call-update) | async-done | bytes 2359312 | tf_op jit(solution)/shard_map/psum | solution.py:300
  737.2 13.4 %convolution_convert_fusion.2 = bf16[1024,3072]{1,0:T(8,128)(2,1)} fusion(bf16[1032,1024]{1,0:T(8,128)(2,1)} %add_convert_fusion.5, bf16[1032,3072]{1,0:T(8,128)(2,1)} %bitcast.222), kind=kOutput, calls=%fused_computation.17 | convolution fusion | flops 6495928320 | bytes 14745600 | tf_op jit(solution)/shard_map/dot_general | solution.py:283
  753.6 13.2 %multiply_reduce_fusion.3 = (f32[1024]{0:T(1024)S(1)}, f32[1032]{0:T(1024)S(1)}, f32[1024]{0:T(1024)S(1)}, f32[1032,1024]{1,0:T(8,128)S(1)}) fusion(f32[1032]{0:T(1024)S(1)} %copy-done.33, f32[1032]{0:T(1024)S(1)} %copy-done.31, bf16[3,344,1024]{2,1,0:T(8,128)(2,1)S(1)} %copy-done.13, f32[1024]{0:T(1024)S(1)} %bitcast.237, ...), kind=kOutput, calls=%fused_computation.27 | convolution fusion | flops 6504403968 | bytes 21110880 | tf_op jit(solution)/shard_map/dot_general | solution.py:321
  772.7 21.2 %multiply_reduce_fusion = (f32[1024]{0:T(1024)S(1)}, f32[1024]{0:T(1024)S(1)}, bf16[1032,1024]{1,0:T(8,128)(2,1)}, bf16[1032,1024]{1,0:T(8,128)(2,1)}) fusion(bf16[3,344,1024]{2,1,0:T(8,128)(2,1)S(1)} %copy-done.15, f32[1032]{0:T(1024)S(1)} %copy-done.27, f32[1032,1024]{1,0:T(8,128)} %get-tuple-element.153, f32[1032,1024]{1,0:T(8,128)} %copy-done.16, ...), kind=kOutput, calls=%fused_computation.21 | convolution fusion | flops 8673949696 | bytes 40120416 | tf_op jit(solution)/shard_map/dot_general | solution.py:260
  793.9 17.7 %reduce-scatter.11.cloned.1.call-done = bf16[128,3072]{1,0:T(8,128)(2,1)} async-done(((bf16[1024,3072]{1,0:T(8,128)(2,1)}), bf16[128,3072]{1,0:T(8,128)(2,1)}) %reduce-scatter.11.cloned.1.call-update) | async-done | bytes 786448 | tf_op jit(solution)/shard_map/reduce_scatter | solution.py:284
  814.2 3.9 convert_reduce_fusion.1
  822.1 40.0 %psum.39 = f32[14,1024]{1,0:T(8,128)S(1)} all-reduce(f32[14,1024]{1,0:T(8,128)S(1)} %concatenate.35), channel_id=1, replica_groups=mesh['img'=8,'seq'=4] {'img','seq'}, use_global_device_ids=true, to_apply=%region_26.27 | all-reduce | flops 14336 | bytes 114688 | tf_op jit(solution)/shard_map/psum | solution.py:341
  (219 shorter events, 87.5 us)
Async XLA Ops:
  7.2 4.2 copy-start.11
  7.2 52.7 %all-gather.7.cloned.1.call-start = ((), (), s32[]{:S(2)}) async-start(), calls=%async_computation.16 | async-start | bytes 7077888 | tf_op jit(solution)/shard_map/all_gather | solution.py:223
  9.9 286.4 %all-gather.9.cloned.1.call-start = ((), (), s32[]{:S(2)}) async-start(), calls=%async_computation.17 | async-start | bytes 2359296 | tf_op jit(solution)/shard_map/all_gather | solution.py:224
  10.7 299.0 %all-gather.11.cloned.1.call-start = ((), (), s32[]{:S(2)}) async-start(), calls=%async_computation.18 | async-start | bytes 9437184 | tf_op jit(solution)/shard_map/all_gather | solution.py:225
  11.9 53.4 %copy-start.30 = (f32[1032]{0:T(1024)}, f32[1032]{0:T(1024)S(1)}, u32[]{:S(2)}) copy-start(f32[1032]{0:T(1024)S(1)} %div.39) | copy-start | bytes 12388
  12.7 52.6 %copy-start.32 = (f32[1032]{0:T(1024)}, f32[1032]{0:T(1024)S(1)}, u32[]{:S(2)}) copy-start(f32[1032]{0:T(1024)S(1)} %rsqrt.20) | copy-start | bytes 12388
  24.4 40.9 %copy-start.38 = (f32[1,8,128]{2,0,1:T(1,128)}, f32[1,8,128]{2,0,1:T(1,128)S(1)}, u32[]{:S(2)}) copy-start(f32[1,8,128]{2,0,1:T(1,128)S(1)} %get-tuple-element.145) | copy-start | bytes 12292
  67.1 53.6 %all-to-all-start.4 = ((bf16[4,344,768]{2,1,0:T(8,128)(2,1)}), bf16[4,344,768]{2,1,0:T(8,128)(2,1)S(1)}, u32[]{:S(2)}, u32[]{:S(2)}) async-start(bf16[4,344,768]{2,1,0:T(8,128)(2,1)} %pad_maximum_fusion.3), calls=%async_computation.4 | async-start | bytes 4227072 | tf_op jit(solution)/shard_map/all_to_all | solution.py:240
  71.7 261.0 %all-gather.13.cloned.1.call-start = ((), (), s32[]{:S(2)}) async-start(), calls=%async_computation.19 | async-start | bytes 9437184 | tf_op jit(solution)/shard_map/all_gather | solution.py:226
  120.6 110.3 %copy-start = (bf16[4,344,768]{2,1,0:T(8,128)(2,1)}, bf16[4,344,768]{2,1,0:T(8,128)(2,1)S(1)}, u32[]{:S(2)}) copy-start(bf16[4,344,768]{2,1,0:T(8,128)(2,1)S(1)} %all-to-all-done.4) | copy-start | bytes 6340612
  120.6 52.6 %all-to-all-start = ((bf16[4,344,768]{2,1,0:T(8,128)(2,1)}), bf16[4,344,768]{2,1,0:T(8,128)(2,1)}, u32[]{:S(2)}, u32[]{:S(2)}) async-start(bf16[4,344,768]{2,1,0:T(8,128)(2,1)} %pad_maximum_fusion.1), calls=%async_computation | async-start | bytes 4227072 | tf_op jit(solution)/shard_map/all_to_all | solution.py:240
  130.7 47.5 %copy-start.40 = (s32[3,1376]{1,0:T(4,128)S(1)}, s32[3,1376]{1,0:T(4,128)}, u32[]{:S(2)}) copy-start(s32[3,1376]{1,0:T(4,128)} %param.15) | copy-start | bytes 49540
  173.3 52.8 %all-to-all-start.2 = ((bf16[4,344,768]{2,1,0:T(8,128)(2,1)}), bf16[4,344,768]{2,1,0:T(8,128)(2,1)}, u32[]{:S(2)}, u32[]{:S(2)}) async-start(bf16[4,344,768]{2,1,0:T(8,128)(2,1)} %pad_maximum_fusion.2), calls=%async_computation.2 | async-start | bytes 4227072 | tf_op jit(solution)/shard_map/all_to_all | solution.py:240
  179.0 13.3 %copy-start.1 = (f32[1376,1]{1,0:T(8,128)}, f32[1376,1]{1,0:T(8,128)S(1)}, u32[]{:S(2)}) copy-start(f32[1376,1]{1,0:T(8,128)S(1)} %copy.47.bias_ref) | copy-start | bytes 16516
  226.0 21.8 %all-to-all-start.1 = ((bf16[4,344,256]{2,1,0:T(8,128)(2,1)}), bf16[4,344,256]{2,1,0:T(8,128)(2,1)S(1)}, u32[]{:S(2)}, u32[]{:S(2)}) async-start(bf16[4,344,256]{2,1,0:T(8,128)(2,1)} %bitcast.19), calls=%async_computation.1 | async-start | bytes 1409024 | tf_op jit(solution)/shard_map/all_to_all | solution.py:245
  247.8 22.3 %all-to-all-start.5 = ((bf16[4,344,256]{2,1,0:T(8,128)(2,1)}), bf16[4,344,256]{2,1,0:T(8,128)(2,1)}, u32[]{:S(2)}, u32[]{:S(2)}) async-start(bf16[4,344,256]{2,1,0:T(8,128)(2,1)} %bitcast.43), calls=%async_computation.5 | async-start | bytes 1409024 | tf_op jit(solution)/shard_map/all_to_all | solution.py:245
  253.6 116.5 %copy-start.26 = (f32[1032]{0:T(1024)}, f32[1032]{0:T(1024)S(1)}, u32[]{:S(2)}) copy-start(f32[1032]{0:T(1024)S(1)} %mul.253) | copy-start | bytes 12388
  254.6 13.3 %copy-start.3 = (f32[1376,1]{1,0:T(8,128)}, f32[1376,1]{1,0:T(8,128)S(1)}, u32[]{:S(2)}) copy-start(f32[1376,1]{1,0:T(8,128)S(1)} %copy.48.bias_ref) | copy-start | bytes 16516
  254.6 19.7 %copy-start.36 = (f32[1,8,128]{2,0,1:T(1,128)S(1)}, f32[1,8,128]{2,0,1:T(1,128)}, u32[]{:S(2)}) copy-start(f32[1,8,128]{2,0,1:T(1,128)} %get-tuple-element.137) | copy-start | bytes 12292
  268.0 12.0 %copy-start.9 = (f32[1376,256]{1,0:T(8,128)}, f32[1376,256]{1,0:T(8,128)S(1)}, u32[]{:S(2)}) copy-start(f32[1376,256]{1,0:T(8,128)S(1)} %get-tuple-element.33.log_ref) | copy-start | bytes 4227076
  270.1 22.1 %all-to-all-start.3 = ((bf16[4,344,256]{2,1,0:T(8,128)(2,1)}), bf16[4,344,256]{2,1,0:T(8,128)(2,1)}, u32[]{:S(2)}, u32[]{:S(2)}) async-start(bf16[4,344,256]{2,1,0:T(8,128)(2,1)} %bitcast.31), calls=%async_computation.3 | async-start | bytes 1409024 | tf_op jit(solution)/shard_map/all_to_all | solution.py:245
  274.3 276.2 %reduce-scatter.9.cloned.1.call-start = ((), (), s32[]{:S(2)}) async-start(), calls=%async_computation.22 | async-start | bytes 2359296 | tf_op jit(solution)/shard_map/reduce_scatter | solution.py:284
  280.8 14.0 %copy-start.18 = (bf16[1,344,1024]{2,1,0:T(8,128)(2,1)S(1)}, bf16[1,344,1024]{2,1,0:T(8,128)(2,1)}, u32[]{:S(2)}) copy-start(bf16[1,344,1024]{2,1,0:T(8,128)(2,1)} %maximum_bitcast_fusion.5) | copy-start | bytes 2113540
  280.8 15.5 %copy-start.12 = (bf16[3,344,1024]{2,1,0:T(8,128)(2,1)S(1)}, bf16[3,344,1024]{2,1,0:T(8,128)(2,1)}, u32[]{:S(2)}) copy-start(bf16[3,344,1024]{2,1,0:T(8,128)(2,1)} %param.13) | copy-start | bytes 6340612
  280.8 15.5 %copy-start.44 = (f32[1,8,128]{2,0,1:T(1,128)S(1)}, f32[1,8,128]{2,0,1:T(1,128)}, u32[]{:S(2)}) copy-start(f32[1,8,128]{2,0,1:T(1,128)} %get-tuple-element.146) | copy-start | bytes 12292
  280.8 15.5 %copy-start.52 = (f32[1,8,128]{2,0,1:T(1,128)S(1)}, f32[1,8,128]{2,0,1:T(1,128)}, u32[]{:S(2)}) copy-start(f32[1,8,128]{2,0,1:T(1,128)} %get-tuple-element.141) | copy-start | bytes 12292
  304.3 5.3 copy-start.45
  304.3 5.3 copy-start.47
  304.3 5.3 copy-start.51
  309.7 23.0 %copy-start.19 = (bf16[1032,1024]{1,0:T(8,128)(2,1)S(1)}, bf16[1032,1024]{1,0:T(8,128)(2,1)}, u32[]{:S(2)}) copy-start(bf16[1032,1024]{1,0:T(8,128)(2,1)} %multiply_convert_fusion.3) | copy-start | bytes 6340612
  377.8 172.7 %reduce-scatter.7.cloned.1.call-start = ((), (), s32[]{:S(2)}) async-start(), calls=%async_computation.21 | async-start | bytes 9437184 | tf_op jit(solution)/shard_map/reduce_scatter | solution.py:284
  395.9 171.3 %reduce-scatter.5.cloned.1.call-start = ((), (), s32[]{:S(2)}) async-start(), calls=%async_computation.20 | async-start | bytes 9437184 | tf_op jit(solution)/shard_map/reduce_scatter | solution.py:284
  420.2 47.3 %copy-start.2 = (f32[1376,1]{1,0:T(8,128)S(1)}, f32[1376,1]{1,0:T(8,128)}, u32[]{:S(2)}) copy-start(f32[1376,1]{1,0:T(8,128)} %copy-done.1) | copy-start | bytes 16516
  421.1 21.1 %all-to-all-start.6 = ((bf16[4,344,256]{2,1,0:T(8,128)(2,1)}), bf16[4,344,256]{2,1,0:T(8,128)(2,1)S(1)}, u32[]{:S(2)}, u32[]{:S(2)}) async-start(bf16[4,344,256]{2,1,0:T(8,128)(2,1)} %pad_maximum_fusion.5), calls=%async_computation.6 | async-start | bytes 1409024 | tf_op jit(solution)/shard_map/all_to_all | solution.py:295
  442.3 21.3 %all-to-all-start.10 = ((bf16[4,344,256]{2,1,0:T(8,128)(2,1)}), bf16[4,344,256]{2,1,0:T(8,128)(2,1)S(1)}, u32[]{:S(2)}, u32[]{:S(2)}) async-start(bf16[4,344,256]{2,1,0:T(8,128)(2,1)} %pad_maximum_fusion.7), calls=%async_computation.10 | async-start | bytes 1409024 | tf_op jit(solution)/shard_map/all_to_all | solution.py:295
  463.6 30.3 %all-to-all-start.8 = ((bf16[4,344,256]{2,1,0:T(8,128)(2,1)}), bf16[4,344,256]{2,1,0:T(8,128)(2,1)S(1)}, u32[]{:S(2)}, u32[]{:S(2)}) async-start(bf16[4,344,256]{2,1,0:T(8,128)(2,1)} %pad_maximum_fusion.6), calls=%async_computation.8 | async-start | bytes 1409024 | tf_op jit(solution)/shard_map/all_to_all | solution.py:295
  493.9 5.3 copy-start.4
  493.9 52.7 %all-to-all-start.7 = ((bf16[4,344,768]{2,1,0:T(8,128)(2,1)}), bf16[4,344,768]{2,1,0:T(8,128)(2,1)}, u32[]{:S(2)}, u32[]{:S(2)}) async-start(bf16[4,344,768]{2,1,0:T(8,128)(2,1)} %bitcast.63), calls=%async_computation.7 | async-start | bytes 4227072 | tf_op jit(solution)/shard_map/all_to_all | solution.py:307
  546.7 51.6 %all-to-all-start.9 = ((bf16[4,344,768]{2,1,0:T(8,128)(2,1)}), bf16[4,344,768]{2,1,0:T(8,128)(2,1)S(1)}, u32[]{:S(2)}, u32[]{:S(2)}) async-start(bf16[4,344,768]{2,1,0:T(8,128)(2,1)} %bitcast.74), calls=%async_computation.9 | async-start | bytes 4227072 | tf_op jit(solution)/shard_map/all_to_all | solution.py:307
  598.3 90.8 %all-to-all-start.11 = ((bf16[4,344,768]{2,1,0:T(8,128)(2,1)}), bf16[4,344,768]{2,1,0:T(8,128)(2,1)}, u32[]{:S(2)}, u32[]{:S(2)}) async-start(bf16[4,344,768]{2,1,0:T(8,128)(2,1)} %bitcast.85), calls=%async_computation.14 | async-start | bytes 4227072 | tf_op jit(solution)/shard_map/all_to_all | solution.py:307
  602.7 134.5 %all-reduce.6.cloned.1.call-start = ((), (), s32[]{:S(2)}) async-start(), calls=%async_computation.25 | async-start | bytes 4718592 | tf_op jit(solution)/shard_map/psum | solution.py:300
  603.5 208.2 %reduce-scatter.11.cloned.1.call-start = ((), (), s32[]{:S(2)}) async-start(), calls=%async_computation.23 | async-start | bytes 7077888 | tf_op jit(solution)/shard_map/reduce_scatter | solution.py:284
  750.7 112.7 %all-reduce.4.cloned.1.call-start = ((), (), s32[]{:S(2)}) async-start(), calls=%async_computation.24 | async-start | bytes 1572864 | tf_op jit(solution)/shard_map/psum | solution.py:324
  753.6 13.2 %copy-start.29 = (f32[1032]{0:T(1024)S(1)}, f32[1032]{0:T(1024)}, u32[]{:S(2)}) copy-start(f32[1032]{0:T(1024)} %copy-done.28) | copy-start | bytes 12388
  813.2 4.9 copy-start.25
  814.1 4.8 copy-start.24
  814.1 6.3 copy-start.23
  818.0 4.0 copy-start.46
  (32 other events, 80.1 us)
Sparse Core Ops, SparseCore 0:
  10.5 49.3 all-gather.6
  61.8 27.8 all-gather.8
  91.6 54.3 all-gather.10
  147.8 54.3 all-gather.12
  377.9 39.5 reduce-scatter.8
  421.2 71.2 reduce-scatter.6
  496.0 71.2 reduce-scatter.4
  606.3 130.8 all-reduce.5
  750.8 60.7 reduce-scatter.10
  814.5 43.9 all-reduce.3
where the time goes:
time: 883 us; the launch traced here: 873 us
  waiting for transfers between devices  386 us (44%)
  matrix products  173 us (20%)
  Pallas kernels  114 us (13%)
  starting transfers between devices  51.1 us (6%)
  other arithmetic  50.5 us (6%)
  blocking collectives  50.5 us (6%)
  local copies, waits for them, and re-layouts  32.1 us (4%)
  between operations  15.2 us (2%)
    all_to_all x3, waiting for transfers between devices, body(): spread = lax.all_to_all(qkv, 'seq', split_axis=0, concat_axis=0, tiled=True)  115 us
    all_to_all x3, waiting for transfers between devices, body(): lax.all_to_all(grad_spread.reshape(seq_count, local_rows, group), 'seq',...  107 us
    pallas_call x3, Pallas kernels, attend_back(): pl.pallas_call(attend_back_kernel, out_shape=jax.ShapeDtypeStruct((seq_le...  76 us
    dot_general x4, matrix products, owned(): jnp.dot(left.T, right, preferred_element_type=jnp.float32)  54.1 us
    psum x1, waiting for transfers between devices, body(): lax.psum((grad_w_down, grad_w_up, grad_w_out), 'seq')  42.7 us
    psum x1, blocking collectives, body(): smalls = lax.psum(smalls, ('img', 'seq'))  40 us
    pallas_call x3, Pallas kernels, attend(): pl.pallas_call(attend_kernel, out_shape=(jax.ShapeDtypeStruct((seq_len, w...  38.1 us
    reduce_scatter x4, waiting for transfers between devices, owned(): return lax.psum_scatter(grad, 'img', scatter_dimension=0, tiled=True)  34.5 us
  transfers between devices with their start and end apart: 22, of which 15 were waited for; matrix products, arithmetic and copies ran while one was open for 21% of the time, Pallas kernels for 13%

commit v1 on v0

v1 whole, which is shorter than its diff:
```python
import jax
import jax.numpy as jnp
from jax import lax
from jax.experimental import pallas as pl
from jax.experimental.pallas import tpu as pltpu
from jax.sharding import Mesh
from jax.sharding import PartitionSpec as P

HD = 64
PAIR = 2 * HD


norm_eps = 1e-06


def norm_rows(values, gain, shift):
    center = values - jnp.mean(values, axis=-1, keepdims=True)
    spread = jnp.mean(center * center, axis=-1, keepdims=True)
    return center * lax.rsqrt(spread + norm_eps) * gain + shift


def gelu_and_slope(values):
    half = 0.5 + 0.5 * lax.erf(values * 0.5**0.5)
    slope = half + values * jnp.exp(-0.5 * values * values) * (0.5 / jnp.pi) ** 0.5
    return (values * half).astype(jnp.bfloat16), slope


def chunks_of(total):
    cuts = list(range(0, total, 512)) + [total]
    return [(cuts[n], cuts[n + 1] - cuts[n]) for n in range(len(cuts) - 1)]


def lane_of(rows):
    return lax.broadcasted_iota(jnp.int32, (rows, PAIR), 1)


def in_three(values):
    high = values.astype(jnp.bfloat16).astype(jnp.float32)
    rest = values - high
    mid = rest.astype(jnp.bfloat16).astype(jnp.float32)
    return high, mid, rest - mid


def dot_nt(left, right):
    return lax.dot_general(left, right, (((1,), (1,)), ((), ())), preferred_element_type=jnp.float32)


def attend_kernel(qkv_ref, bias_ref, out_ref, log_ref):
    seq_len, width = out_ref.shape
    lane = lane_of(seq_len)
    bias = jnp.broadcast_to(bias_ref[...], (seq_len, PAIR))
    ones = jnp.ones((seq_len, PAIR), jnp.bfloat16)
    key_extra = jnp.where(lane == 0, bias, 0.0).astype(jnp.bfloat16)
    for pair in range(width // PAIR):
        at = pair * PAIR
        keys = qkv_ref[:, 3 * at + PAIR : 3 * at + 2 * PAIR]
        values = qkv_ref[:, 3 * at + 2 * PAIR : 3 * at + 3 * PAIR]
        value_wide = jnp.concatenate([values, ones], axis=1)
        for start, size in chunks_of(seq_len):
            rows = slice(start, start + size)
            first = lane_of(size) < HD
            query = qkv_ref[rows, 3 * at : 3 * at + PAIR] * jnp.bfloat16(0.125)
            query_extra = jnp.where(lane_of(size) == 0, 1.0, 0.0).astype(jnp.bfloat16)
            query_wide = jnp.concatenate([query, query_extra], axis=1)
            parts = []
            for half in range(2):
                own = (lane >= HD) if half else (lane < HD)
                key_own = jnp.where(own, keys.astype(jnp.float32), 0.0).astype(jnp.bfloat16)
                key_wide = jnp.concatenate([key_own, key_extra], axis=1)
                scores = dot_nt(query_wide, key_wide)
                row_max = jnp.max(scores, axis=1, keepdims=True)
                weights = jnp.exp(scores - row_max).astype(jnp.bfloat16)
                mixed = jnp.dot(weights, value_wide, preferred_element_type=jnp.float32)
                total = mixed[:, PAIR:]
                parts.append((mixed[:, :PAIR] / total, row_max + jnp.log(total)))
            out_ref[rows, at : at + PAIR] = jnp.where(first, parts[0][0], parts[1][0]).astype(
                out_ref.dtype
            )
            log_ref[rows, at : at + PAIR] = jnp.where(first, parts[0][1], parts[1][1])


def attend_back_kernel(qkv_ref, bias_ref, log_ref, out_ref, grad_ref, dqkv_ref):
    seq_len = out_ref.shape[0]
    lane = lane_of(seq_len)
    place = lax.rem(lane, HD)
    bias = jnp.broadcast_to(bias_ref[...], (seq_len, PAIR))
    minus = jnp.where(place < 3, -1.0, 0.0)
    key_tail = jnp.where(place == 3, bias, minus)
    query = qkv_ref[:, :PAIR] * jnp.bfloat16(0.125)
    keys = qkv_ref[:, PAIR : 2 * PAIR].astype(jnp.float32)
    values = qkv_ref[:, 2 * PAIR :].astype(jnp.float32)
    grad = grad_ref[...]
    high, mid, low = in_three(log_ref[...])
    tail = jnp.where(place == 0, high, jnp.where(place == 1, mid, low))
    tail = jnp.where(place < 3, tail, jnp.where(place == 3, 1.0, 0.0))
    query_wide = jnp.concatenate([query, tail.astype(jnp.bfloat16)], axis=1)
    product = grad.astype(jnp.float32) * out_ref[...].astype(jnp.float32)
    inner_a = jnp.sum(jnp.where(lane < HD, product, 0.0), axis=1, keepdims=True)
    inner_b = jnp.sum(jnp.where(lane < HD, 0.0, product), axis=1, keepdims=True)
    high, mid, low = in_three(jnp.where(lane < HD, inner_a, inner_b))
    tail = jnp.where(place == 0, high, jnp.where(place == 1, mid, low))
    tail = jnp.where(place < 3, tail, 0.0)
    grad_wide = jnp.concatenate([grad, tail.astype(jnp.bfloat16)], axis=1)
    total_q = [None, None]
    for start, size in chunks_of(seq_len):
        rows = slice(start, start + size)
        first = lane_of(size) < HD
        keys_here = keys[rows].astype(jnp.bfloat16)
        parts = []
        for half in range(2):
            own = jnp.logical_not(first) if half else first
            key_wide = jnp.concatenate(
                [jnp.where(own, keys[rows], 0.0), jnp.where(own, key_tail[rows], 0.0)], axis=1
            ).astype(jnp.bfloat16)
            value_wide = jnp.concatenate(
                [jnp.where(own, values[rows], 0.0), jnp.where(own, minus[rows], 0.0)], axis=1
            ).astype(jnp.bfloat16)
            probs = jnp.exp(dot_nt(key_wide, query_wide))
            grad_scores = (probs * dot_nt(value_wide, grad_wide)).astype(jnp.bfloat16)
            grad_value = jnp.dot(
                probs.astype(jnp.bfloat16), grad, preferred_element_type=jnp.float32
            )
            grad_key = jnp.dot(grad_scores, query, preferred_element_type=jnp.float32)
            part_q = lax.dot_general(
                grad_scores,
                keys_here,
                (((0,), (0,)), ((), ())),
                preferred_element_type=jnp.float32,
            )
            total_q[half] = part_q if total_q[half] is None else total_q[half] + part_q
            parts.append((grad_key, grad_value))
        dqkv_ref[rows, PAIR : 2 * PAIR] = jnp.where(first, parts[0][0], parts[1][0]).astype(
            dqkv_ref.dtype
        )
        dqkv_ref[rows, 2 * PAIR :] = jnp.where(first, parts[0][1], parts[1][1]).astype(
            dqkv_ref.dtype
        )
    dqkv_ref[:, :PAIR] = (jnp.where(lane < HD, total_q[0], total_q[1]) * 0.125).astype(
        dqkv_ref.dtype
    )


def attend(qkv, key_bias):
    seq_len, triple = qkv.shape
    width = triple // 3
    return pl.pallas_call(
        attend_kernel,
        out_shape=(
            jax.ShapeDtypeStruct((seq_len, width), jnp.bfloat16),
            jax.ShapeDtypeStruct((seq_len, width), jnp.float32),
        ),
        cost_estimate=pl.CostEstimate(
            flops=16 * seq_len * seq_len * width,
            bytes_accessed=14 * seq_len * width,
            transcendentals=seq_len * seq_len * width // HD,
        ),
        compiler_params=pltpu.CompilerParams(vmem_limit_bytes=48 * 1024 * 1024),
        name="attend",
    )(qkv, key_bias)


def attend_back(pair, qkv, key_bias, log_total, mixed, grad_mixed):
    seq_len = qkv.shape[0]
    one = pl.BlockSpec((seq_len, PAIR), lambda i: (0, pair))
    return pl.pallas_call(
        attend_back_kernel,
        grid=(1,),
        in_specs=[
            pl.BlockSpec((seq_len, 3 * PAIR), lambda i: (0, pair)),
            pl.BlockSpec((seq_len, 1), lambda i: (0, 0)),
            one,
            one,
            one,
        ],
        out_specs=pl.BlockSpec((seq_len, 3 * PAIR), lambda i: (0, 0)),
        out_shape=jax.ShapeDtypeStruct((seq_len, 3 * PAIR), jnp.bfloat16),
        cost_estimate=pl.CostEstimate(
            flops=40 * seq_len * seq_len * PAIR,
            bytes_accessed=20 * seq_len * PAIR,
            transcendentals=seq_len * seq_len * PAIR // HD,
        ),
        compiler_params=pltpu.CompilerParams(vmem_limit_bytes=48 * 1024 * 1024),
        name="attend_back",
    )(qkv, key_bias, log_total, mixed, grad_mixed)


HOME = ("core", "low")
IMG = ("chip", "core")
SEQ = ("high", "low")


def traded(values):
    moved = lax.ppermute(values, ("core", "high"), [(1, 2), (2, 1)])
    return jnp.where(lax.axis_index("core") == lax.axis_index("high"), values, moved)


def swapped(values, axis, bit=1):
    count = lax.axis_size(axis)
    return lax.ppermute(values, axis, [(n, n ^ bit) for n in range(count)])


def summed(values):
    for axis in ("core", "low", "chip", "high"):
        bit = 1
        while bit < lax.axis_size(axis):
            values = values + swapped(values, axis, bit)
            bit *= 2
    return values


def summed_seq(values):
    if lax.axis_size("low") != 2:
        return lax.psum(values, SEQ).astype(jnp.float32)
    rows = values.shape[0] // 2
    low = lax.axis_index("low")
    mine = lax.dynamic_slice_in_dim(values, low * rows, rows, 0)
    other = lax.dynamic_slice_in_dim(values, (1 - low) * rows, rows, 0)
    mine = mine + swapped(other, "low")
    mine = mine + swapped(mine, "high")
    other = swapped(mine, "low")
    first = jnp.where(low == 0, mine, other)
    second = jnp.where(low == 0, other, mine)
    return jnp.concatenate([first, second], axis=0).astype(jnp.float32)


def rows_of(left):
    chips = lax.axis_size("chip")
    chip, core = lax.axis_index("chip"), lax.axis_index("core")
    part = left.shape[1] // (2 * chips)

    def side_of(side):
        order = [chip ^ (1 + side), chip ^ 3, chip ^ (2 - side), chip]
        order = order if chips == 4 else range(chips)
        picked = [lax.dynamic_slice_in_dim(left, (n * 2 + side) * part, part, 1) for n in order]
        return jnp.concatenate(picked, axis=1)

    return lax.optimization_barrier((side_of(1 - core), side_of(core)))


def product(left, right):
    return lax.dot_general(
        left, right, (((0,), (0,)), ((), ())), preferred_element_type=jnp.float32
    ).astype(jnp.bfloat16)


def products(rows, right):
    return product(rows[0], right), product(rows[1], right)


def owned(send, keep):
    chips = lax.axis_size("chip")
    total = keep + swapped(send, "core")
    if chips != 4:
        total = lax.psum_scatter(total, "chip", scatter_dimension=0, tiled=True)
        return summed_seq(total)
    total = total.reshape(chips, -1, total.shape[1])
    first = [(n * 2 + c, (n ^ (1 + c)) * 2 + c) for n in range(chips) for c in range(2)]
    second = [(n * 2 + c, (n ^ (2 - c)) * 2 + c) for n in range(chips) for c in range(2)]
    came = lax.ppermute(total[:2], IMG, first)
    onward = total[2] + came[1]
    total = total[3] + came[0] + lax.ppermute(onward, IMG, second)
    return summed_seq(total)


def body(
    tokens,
    cotangent,
    token_mask,
    slot_flags,
    w_qkv,
    w_out,
    w_up,
    w_down,
    norm_gain,
    norm_bias,
    proj_bias,
    up_bias,
    layer_scale,
):
    seq_count = lax.axis_size(HOME)
    seq_place = lax.axis_index(HOME)
    img_count = lax.axis_size(IMG)
    img_place = lax.axis_index(IMG)
    images, local_rows, model_width = tokens.shape
    seq_len = token_mask.shape[1]
    head_cols = model_width // seq_count
    pairs = head_cols // PAIR
    shard = norm_gain.shape[1]
    up_rows = up_bias.shape[0] // shard

    facts = traded(jnp.concatenate([jnp.sum(token_mask, axis=1), slot_flags]))
    lengths, flags = facts[:images], facts[images:]
    here = lax.broadcasted_iota(jnp.int32, (images, local_rows), 1) + seq_place * local_rows
    live_rows = ((here < lengths[:, None]) & (flags[:, None] > 0)).astype(jnp.float32)
    live_rows = live_rows.reshape(-1, 1)
    place = lax.broadcasted_iota(jnp.int32, (images, seq_len, 1), 1)
    place = place + ((place // local_rows) ^ seq_place) * local_rows - place // local_rows * local_rows
    key_bias = jnp.where(place < lengths[:, None, None], 0.0, -1e30).astype(jnp.float32)

    def by_pair(matrix):
        rows = matrix.shape[0]
        split = matrix.reshape(rows, 3, seq_count, pairs, PAIR)
        return split.transpose(0, 3, 2, 1, 4).reshape(rows, -1)

    def by_kind(matrix):
        rows = matrix.shape[0]
        split = matrix.reshape(rows, pairs, seq_count, 3, PAIR)
        return split.transpose(0, 3, 2, 1, 4).reshape(rows, -1)

    def to_heads(matrix, runs=1):
        width = matrix.shape[1] // (seq_count * runs)
        parts = []
        for n in range(seq_count):
            part = [
                lax.dynamic_slice_in_dim(
                    matrix, (run * seq_count + (seq_place ^ n)) * width, width, 1
                )
                for run in range(runs)
            ]
            part = jnp.concatenate(part, axis=1)
            parts.append(swapped(part, HOME, n) if n else part)
        return jnp.concatenate(parts, axis=0)

    def to_tokens(block):
        parts = []
        for n in range(seq_count):
            part = block[n * local_rows : (n + 1) * local_rows]
            parts.append(swapped(part, HOME, n) if n else part)
        return parts

    def laid(slots):
        width = slots[0][0].shape[1]
        whole = jnp.zeros((images * local_rows, seq_count * width), jnp.bfloat16)
        for slot, parts in enumerate(slots):
            for n, part in enumerate(parts):
                whole = lax.dynamic_update_slice(
                    whole, part, (slot * local_rows, (seq_place ^ n) * width)
                )
        return whole

    small = jnp.concatenate(
        [norm_gain, norm_bias, proj_bias, layer_scale, up_bias.reshape(up_rows, shard)], axis=0
    )
    small = lax.all_gather(small, IMG, axis=0, tiled=False).astype(jnp.float32)
    up_bias_f = small[:, 10:].reshape(-1)
    small = small.swapaxes(0, 1).reshape(-1, model_width)
    gain_f, shift_f, bias_f, scale_f = (small[0:2], small[2:4], small[4:8], small[8:10])
    qkv_full = lax.all_gather(by_pair(w_qkv), IMG, axis=0, tiled=True)
    out_full = lax.all_gather(w_out, IMG, axis=0, tiled=True)
    up_full = lax.all_gather(w_up, IMG, axis=0, tiled=True)
    down_full = lax.all_gather(w_down, IMG, axis=0, tiled=True)

    tokens = jnp.stack([traded(tokens[slot]) for slot in range(images)])
    inputs = tokens.reshape(-1, model_width).astype(jnp.float32)
    normed_one, norm_one_pulls = [], []
    for slot in range(images):
        normed, pull = jax.vjp(norm_rows, tokens[slot].astype(jnp.float32), gain_f[0], shift_f[0])
        normed_one.append(normed.astype(jnp.bfloat16))
        norm_one_pulls.append(pull)
    rows_one = rows_of(jnp.concatenate(normed_one, axis=0))
    shift_qkv = jnp.concatenate([bias_f[0], jnp.zeros((model_width,), jnp.float32), bias_f[1]])
    shift_qkv = by_pair(shift_qkv[None])
    saved = []
    returned = []
    for slot in range(images):
        qkv = jnp.dot(normed_one[slot], qkv_full, preferred_element_type=jnp.float32)
        qkv = (qkv + shift_qkv).astype(jnp.bfloat16)
        spread = to_heads(qkv, pairs)
        mixed, log_total = attend(spread, key_bias[slot])
        saved.append((spread, key_bias[slot], log_total, mixed))
        returned.append(to_tokens(mixed))
    last, cotangent = lax.optimization_barrier((saved[-1][0], cotangent))
    saved[-1] = (last,) + saved[-1][1:]
    cotangent = traded(cotangent)
    attended = laid(returned)
    branch = jnp.dot(attended, out_full, preferred_element_type=jnp.float32) + bias_f[2]
    middle = inputs + scale_f[0] * branch
    normed_two, norm_two_pull = jax.vjp(norm_rows, middle, gain_f[1], shift_f[1])
    normed_two = normed_two.astype(jnp.bfloat16)
    up_proj = jnp.dot(normed_two, up_full, preferred_element_type=jnp.float32) + up_bias_f
    activated, gelu_slope = lax.optimization_barrier(gelu_and_slope(up_proj))
    grad_y = cotangent.reshape(-1, model_width).astype(jnp.float32) * live_rows
    grad_down = (grad_y * scale_f[1]).astype(jnp.bfloat16)
    grad_bias_down = jnp.sum(grad_down.astype(jnp.float32), axis=0)
    barrier = lax.optimization_barrier
    grad_down, grad_w_down = barrier((grad_down, product(activated, grad_down)))
    grad_w_down = lax.psum_scatter(grad_w_down, IMG, scatter_dimension=0, tiled=True)
    grad_act = jnp.dot(grad_down, down_full.T, preferred_element_type=jnp.float32)
    grad_up = (grad_act * gelu_slope).astype(jnp.bfloat16)
    grad_up_bias = jnp.sum(grad_up.astype(jnp.float32), axis=0)
    grad_up, grad_w_up = barrier((grad_up, product(normed_two, grad_up)))
    grad_w_up = lax.psum_scatter(grad_w_up, IMG, scatter_dimension=0, tiled=True)
    grad_normed_two = jnp.dot(grad_up, up_full.T, preferred_element_type=jnp.float32)
    grad_from_two, grad_gain_two, grad_shift_two = norm_two_pull(grad_normed_two)
    grad_middle = grad_y + grad_from_two
    grad_scale_one = jnp.sum(grad_middle * branch, axis=0)
    grad_branch = (grad_middle * scale_f[0]).astype(jnp.bfloat16)
    grad_bias_out = jnp.sum(grad_branch.astype(jnp.float32), axis=0)
    grad_attended = jnp.dot(grad_branch, out_full.T, preferred_element_type=jnp.float32).astype(
        jnp.bfloat16
    )
    grad_attended = grad_attended.reshape(images, local_rows, model_width)

    grad_w_out = products(rows_of(attended), grad_branch)
    grads_mixed = [to_heads(grad_attended[slot]) for slot in range(images)]
    grad_parts = []
    grad_w_qkv = []
    for pair in range(pairs):
        grad_slots = []
        for slot in range(images):
            spread, slot_bias, log_total, mixed = saved[slot]
            if pair == 0 and slot == 0:
                spread, grad_w_out = barrier((spread, grad_w_out))
            if pair and slot == images - 1:
                earlier = barrier((grad_parts[-1], grad_slots))
                grad_parts[-1] = laid(earlier[0])
                grad_slots = earlier[1]
                grad_w_qkv.append(products(rows_one, grad_parts[-1]))
                spread, grad_w_qkv[-1] = barrier((spread, grad_w_qkv[-1]))
            last = attend_back(pair, spread, slot_bias, log_total, mixed, grads_mixed[slot])
            if slot == images - 1 and pair == pairs - 1:
                last, activated = barrier((last, activated))
            grad_slots.append(to_tokens(last))
        grad_parts.append(grad_slots)
    grad_parts[-1] = laid(grad_parts[-1])
    grad_w_qkv.append(products(rows_one, grad_parts[-1]))
    grad_w_down, grad_w_up = (
        grad.astype(jnp.float32) for grad in lax.psum((grad_w_down, grad_w_up), SEQ)
    )
    grad_w_qkv[0] = [
        jnp.concatenate(both, axis=1) for both in zip(grad_w_qkv[0], grad_w_out, strict=True)
    ]
    grad_w_qkv = jnp.concatenate([owned(*both) for both in grad_w_qkv], axis=1)
    cut = 3 * seq_count * PAIR
    grad_w_out = grad_w_qkv[:, cut : cut + model_width]
    grad_w_qkv = jnp.concatenate([grad_w_qkv[:, :cut], grad_w_qkv[:, cut + model_width :]], axis=1)
    grad_w_qkv = by_kind(grad_w_qkv)

    down_proj = jnp.dot(activated, down_full, preferred_element_type=jnp.float32) + bias_f[3]
    result = (
        ((middle + scale_f[1] * down_proj) * live_rows).astype(jnp.bfloat16).reshape(tokens.shape)
    )
    result = traded(result)
    grad_scale_two = jnp.sum(grad_y * down_proj, axis=0)
    grad_inputs, grad_gain_one, grad_shift_one = [], 0.0, 0.0
    for slot in range(images):
        rows = slice(slot * local_rows, (slot + 1) * local_rows)
        grad_normed = 0.0
        for pair in range(pairs):
            cols = slice(pair * seq_count * 3 * PAIR, (pair + 1) * seq_count * 3 * PAIR)
            grad_normed += lax.dot_general(
                grad_parts[pair][rows],
                qkv_full[:, cols],
                (((1,), (1,)), ((), ())),
                preferred_element_type=jnp.float32,
            )
        grad_from_one, grad_gain, grad_shift = norm_one_pulls[slot](grad_normed)
        grad_inputs.append(traded((grad_middle[rows] + grad_from_one).astype(jnp.bfloat16)))
        grad_gain_one += grad_gain
        grad_shift_one += grad_shift
    grad_inputs = jnp.stack(grad_inputs)
    grad_bias_qkv = [jnp.sum(part.astype(jnp.float32), axis=0) for part in grad_parts]
    grad_bias_qkv = by_kind(jnp.concatenate(grad_bias_qkv)[None])[0]
    smalls = jnp.stack(
        [
            grad_gain_one,
            grad_gain_two,
            grad_shift_one,
            grad_shift_two,
            grad_bias_qkv[:model_width],
            grad_bias_qkv[2 * model_width :],
            grad_bias_out,
            grad_bias_down,
            grad_scale_one,
            grad_scale_two,
        ]
    )
    grad_up_bias = grad_up_bias.reshape(img_count, up_rows, shard).swapaxes(0, 1)
    smalls = jnp.concatenate([smalls, grad_up_bias.reshape(up_rows, model_width)], axis=0)
    smalls = summed(smalls)
    smalls = lax.dynamic_slice_in_dim(smalls, img_place * shard, shard, 1)
    return (
        result,
        grad_inputs,
        grad_w_qkv,
        grad_w_out,
        grad_w_up,
        grad_w_down,
        smalls[0:2],
        smalls[2:4],
        smalls[4:8],
        smalls[10:].reshape(-1),
        smalls[8:10],
    )


def solution(mesh):
    img_count, seq_count = mesh.devices.shape
    split = mesh.devices.reshape(img_count // 2, 2, 2, seq_count // 2)
    mesh = Mesh(split, IMG + SEQ)
    placed = (
        P(IMG, SEQ, None),
        P(IMG, SEQ, None),
        P(IMG, None),
        P(IMG),
        P(IMG, None),
        P(IMG, None),
        P(IMG, None),
        P(IMG, None),
        P(None, IMG),
        P(None, IMG),
        P(None, IMG),
        P(IMG),
        P(None, IMG),
    )
    return jax.shard_map(
        body,
        mesh=mesh,
        in_specs=placed,
        out_specs=(
            P(IMG, SEQ, None),
            P(IMG, SEQ, None),
            P(IMG, None),
            P(IMG, None),
            P(IMG, None),
            P(IMG, None),
            P(None, IMG),
            P(None, IMG),
            P(None, IMG),
            P(IMG),
            P(None, IMG),
        ),
        check_vma=False,
    )
```

time: 883 us -> 782 us (0.89)
  waiting for transfers between devices: 386 us -> 266 us
  starting transfers between devices: 51.1 us -> 110 us
  blocking collectives: 50.5 us -> 19.4 us
  matrix products: 173 us -> 155 us
  local copies, waits for them, and re-layouts: 32.1 us -> 45.4 us
    all_to_all x12 -> x0, waiting for transfers between devices: 273 us -> none  [the longest x3 115 us: body(): spread = lax.all_to_all(qkv, 'seq', split_axis=0, concat_axis=0, tiled=True)]
    ppermute x0 -> x71, waiting for transfers between devices: none -> 192 us  [the longest x58 167 us: swapped(): return lax.ppermute(values, axis, [(n, n ^ bit) for n in range(count)])]
    ppermute x0 -> x71, starting transfers between devices: none -> 110 us  [the longest x58 95.7 us: swapped(): return lax.ppermute(values, axis, [(n, n ^ bit) for n in range(count)])]
    all_to_all x12 -> x0, starting transfers between devices: 50.7 us -> none  [the longest x3 13.9 us: body(): spread = lax.all_to_all(qkv, 'seq', split_axis=0, concat_axis=0, tiled=True)]
    psum x1 -> x0, blocking collectives: 40 us -> none  [body(): smalls = lax.psum(smalls, ('img', 'seq'))]
    reduce_scatter x4 -> x2, waiting for transfers between devices: 34.5 us -> 0.04 us  [the longest x1 0.02 us: body(): lax.psum_scatter(grad_w_up, IMG, scatter_dimension=0, tiled=True)]
    all_gather x4, waiting for transfers between devices: 33.3 us -> 10.1 us  [the longest x1 10.1 us: body(): qkv_full = lax.all_gather(by_pair(w_qkv), IMG, axis=0, tiled=True)]
    psum x2 -> x1, waiting for transfers between devices: 42.7 us -> 62.7 us  [body(): lax.psum((grad_w_down, grad_w_up), SEQ)]
  transfers between devices with their start and end apart: 22 -> 78, of which waited for: 15 -> 26; matrix products, arithmetic and copies ran while one was open for 21% -> 25% of each run, Pallas kernels for 13% -> 14%
where the time goes in v1:
time: 782 us; the launch traced here: 771 us
  waiting for transfers between devices  266 us (34%)
  matrix products  155 us (20%)
  starting transfers between devices  110 us (14%)
  Pallas kernels  108 us (14%)
  other arithmetic  50.6 us (6%)
  local copies, waits for them, and re-layouts  45.4 us (6%)
  blocking collectives  19.4 us (2%)
  between operations  17 us (2%)
    ppermute x58, waiting for transfers between devices, swapped(): return lax.ppermute(values, axis, [(n, n ^ bit) for n in range(count)])  167 us
    ppermute x58, starting transfers between devices, swapped(): return lax.ppermute(values, axis, [(n, n ^ bit) for n in range(count)])  95.7 us
    pallas_call x6, Pallas kernels, attend_back(): pl.pallas_call(attend_back_kernel, grid=(1,), in_specs=[pl.BlockSpec((seq...  75.7 us
    psum x1, waiting for transfers between devices, body(): lax.psum((grad_w_down, grad_w_up), SEQ)  62.7 us
    dot_general x8, matrix products, product(): lax.dot_general(left, right, (((0,), (0,)), ((), ())), preferred_element_...  49 us
    pallas_call x3, Pallas kernels, attend(): pl.pallas_call(attend_kernel, out_shape=(jax.ShapeDtypeStruct((seq_len, w...  31.9 us
    dot_general x1, matrix products, body(): jnp.dot(normed_two, up_full, preferred_element_type=jnp.float32) + up_bias_f  21.3 us
    unnamed x282, local copies, waits for them, and re-layouts  20.5 us
  transfers between devices with their start and end apart: 78, of which 26 were waited for; matrix products, arithmetic and copies ran while one was open for 25% of the time, Pallas kernels for 14%

profile of v1, /device:TPU:0, one launch (start us, length us, event | category | flops | bytes accessed | tf_op | source)
XLA Modules:
  0.0 771.3 jit_solution(6382753423586227665)
XLA Ops:
  16.8 19.4 %all-gather.1 = bf16[8,14,128]{2,1,0:T(8,128)(2,1)S(1)} all-gather(bf16[1,14,128]{2,1,0:T(8,128)(2,1)S(1)} %bitcast.179), channel_id=2, replica_groups=mesh['chip'=4,'core'=2,'high'=2,'low'=2] {'chip','core'}, dimensions={0}, use_global_device_ids=true | all-gather | bytes 32256 | tf_op jit(solution)/shard_map/all_gather | solution.py:344
  49.8 10.1 %all-gather.7.cloned.1.call-done = bf16[1024,3072]{0,1:T(8,128)(2,1)} async-done(((bf16[128,3072]{0,1:T(8,128)(2,1)}), bf16[1024,3072]{0,1:T(8,128)(2,1)}) %all-gather.7.cloned.1.call-update) | async-done | bytes 6291472 | tf_op jit(solution)/shard_map/all_gather | solution.py:348
  59.9 5.3 add_convert_fusion.3
  67.2 16.2 %collective-permute-start.4 = (bf16[344,768]{1,0:T(8,128)(2,1)S(1)}, bf16[344,768]{1,0:T(8,128)(2,1)S(1)}, u32[]{:S(2)}, u32[]{:S(2)}) collective-permute-start(bf16[344,768]{1,0:T(8,128)(2,1)S(1)} %pad_maximum_fusion.16), channel_id=1, source_target_pairs={{0,4},{1,5},{4,0},{5,1},{2,6},{3,7},{6,2},{7,3},{8,12},{9,13},{12,... | collective-permute-start | bytes 1585160 | tf_op jit(solution)/shard_map/ppermute | solution.py:199
  97.0 9.9 %collective-permute-done.5 = bf16[344,768]{1,0:T(8,128)(2,1)S(1)} collective-permute-done((bf16[344,768]{1,0:T(8,128)(2,1)S(1)}, bf16[344,768]{1,0:T(8,128)(2,1)S(1)}, u32[]{:S(2)}, u32[]{:S(2)}) %collective-permute-start.5) | collective-permute-done | bytes 528416 | tf_op jit(solution)/shard_map/ppermute | solution.py:199
  108.6 10.6 %attend.3 = (bf16[1376,256]{1,0:T(8,128)(2,1)S(1)}, f32[1376,256]{1,0:T(8,128)S(1)}) custom-call(bf16[1376,768]{1,0:T(8,128)(2,1)S(1)} %pad_maximum_fusion.2.qkv_ref, f32[1376,1]{1,0:T(8,128)S(1)} %copy.53.bias_ref), custom_call_target="tpu_custom_call" | custom-call | flops 7755268096 | bytes 4931584 | tf_op jit(solution)/shard_map/attend/pallas_call | solution.py:146
  122.6 6.9 collective-permute-done.12
  131.9 10.6 %attend.4 = (bf16[1376,256]{1,0:T(8,128)(2,1)S(1)}, f32[1376,256]{1,0:T(8,128)S(1)}) custom-call(bf16[1376,768]{1,0:T(8,128)(2,1)S(1)} %pad_maximum_fusion.3.qkv_ref, f32[1376,1]{1,0:T(8,128)S(1)} %copy.54.bias_ref), custom_call_target="tpu_custom_call" | custom-call | flops 7755268096 | bytes 4931584 | tf_op jit(solution)/shard_map/attend/pallas_call | solution.py:146
  142.8 8.7 %collective-permute-done.18 = bf16[344,768]{1,0:T(8,128)(2,1)S(1)} collective-permute-done((bf16[344,768]{1,0:T(8,128)(2,1)S(1)}, bf16[344,768]{1,0:T(8,128)(2,1)S(1)}, u32[]{:S(2)}, u32[]{:S(2)}) %collective-permute-start.18) | collective-permute-done | bytes 528416 | tf_op jit(solution)/shard_map/ppermute | solution.py:199
  156.2 10.6 %attend.5 = (bf16[1376,256]{1,0:T(8,128)(2,1)S(1)}, f32[1376,256]{1,0:T(8,128)S(1)}) custom-call(bf16[1376,768]{1,0:T(8,128)(2,1)S(1)} %pad_maximum_fusion.4.qkv_ref, f32[1376,1]{1,0:T(8,128)S(1)} %copy.55.bias_ref), custom_call_target="tpu_custom_call" | custom-call | flops 7755268096 | bytes 4931584 | tf_op jit(solution)/shard_map/attend/pallas_call | solution.py:146
  168.5 4.6 collective-permute-done.15
  179.8 4.5 collective-permute-start.21
  184.4 6.5 collective-permute-done.21
  194.5 4.9 convolution_add_fusion.2
  209.7 21.3 %fusion.3 = (f32[1032,4096]{1,0:T(8,128)}, bf16[1032,4096]{1,0:T(8,128)(2,1)S(1)}) fusion(f32[4096]{0:T(1024)S(1)} %bitcast.180, bf16[1024,4096]{1,0:T(8,128)(2,1)} %all-gather.11.cloned.1.call-done, f32[1032,1024]{1,0:T(8,128)} %copy-done.20, f32[1024]{0:T(1024)S(1)} %bitcast.190, f32[1024]{0:T(1024)S(1)} %bitcast.170, f32[1032]{0:T(1024)S(1)} %fusion.79, ...), kind=kOutput, calls=%fused_computation.6 | convolution fusion | flops 8708825088 | bytes 38010944 | tf_op jit(solution)/shard_map/dot_general | solution.py:380
  231.0 3.4 copy-done.131
  234.5 13.1 %convolution_convert_fusion = bf16[4096,1024]{1,0:T(8,128)(2,1)} fusion(bf16[1032,4096]{1,0:T(8,128)(2,1)S(1)} %get-tuple-element.87, bf16[1032,1024]{1,0:T(8,128)(2,1)S(1)} %copy-done.45), kind=kOutput, calls=%fused_computation.11 | convolution fusion | flops 8661237760 | bytes 18956288 | tf_op jit(solution)/shard_map/dot_general | solution.py:241
  247.6 17.1 %convert_reduce_fusion = (f32[4096]{0:T(1024)}, bf16[1032,4096]{1,0:T(8,128)(2,1)}) fusion(f32[1032,4096]{1,0:T(8,128)} %get-tuple-element.66, bf16[1032,1024]{1,0:T(8,128)(2,1)} %multiply_convert_fusion.4, bf16[4096,1024]{1,0:T(8,128)(2,1)} %all-gather.13.cloned.1.call-done), kind=kOutput, calls=%fused_computation.7 | convolution fusion | flops 8673947648 | bytes 35880960 | tf_op jit(solution)/shard_map/dot_general | solution.py:388
  264.7 18.1 %convolution_convert_fusion.1 = bf16[1024,4096]{1,0:T(8,128)(2,1)} fusion(bf16[1032,4096]{1,0:T(8,128)(2,1)} %get-tuple-element.67, f32[1032,1024]{1,0:T(8,128)} %copy-done.20, f32[1024]{0:T(1024)S(1)} %bitcast.191, f32[1024]{0:T(1024)S(1)} %bitcast.171, f32[1032]{0:T(1024)S(1)} %fusion.79, f32[1032]{0:T(1024)S(1)} %broadcast_multiply_fusion), kind=kOutput, calls=%fused_computation.12 | convolution fusion | flops 8666521600 | bytes 21086272 | tf_op jit(solution)/shard_map/dot_general | solution.py:241
  282.9 16.8 %multiply_reduce_fusion.2 = (f32[1024]{0:T(1024)}, f32[1032]{0:T(1024)S(1)}, f32[1024]{0:T(1024)}, f32[1032,1024]{1,0:T(8,128)S(1)}) fusion(f32[1032,1024]{1,0:T(8,128)} %copy-done.20, f32[1032]{0:T(1024)S(1)} %fusion.79, f32[1032]{0:T(1024)S(1)} %broadcast_multiply_fusion, f32[1024]{0:T(1024)S(1)} %bitcast.172, bf16[1032,4096]{1,0:T(8,128)(2,1)} %get-tuple-element.67, ...), kind=kOutput, calls=%fused_computation.25 | convolution fusion | flops 8665494528 | bytes 25321568 | tf_op jit(solution)/shard_map/dot_general | solution.py:393
  299.7 3.6 fusion.89
  310.7 23.1 %collective-permute-start.29 = (bf16[344,256]{1,0:T(8,128)(2,1)S(1)}, bf16[344,256]{1,0:T(8,128)(2,1)S(1)}, u32[]{:S(2)}, u32[]{:S(2)}) collective-permute-start(bf16[344,256]{1,0:T(8,128)(2,1)S(1)} %get-tuple-element.267), channel_id=1, source_target_pairs={{0,1},{1,0},{4,5},{5,4},{2,3},{3,2},{6,7},{7,6},{8,9},{9,8},{12,13... | collective-permute-start | bytes 528392 | tf_op jit(solution)/shard_map/ppermute | solution.py:199
  333.7 3.9 collective-permute-start.30
  346.9 12.8 %attend_back.10 = bf16[1376,384]{1,0:T(8,128)(2,1)S(1)} custom-call(bf16[1376,768]{1,0:T(8,128)(2,1)} %copy-done.2, f32[1376,1]{1,0:T(8,128)S(1)} %copy.54.bias_ref, f32[1376,256]{1,0:T(8,128)S(1)} %copy-done.19, bf16[1376,256]{1,0:T(8,128)(2,1)S(1)} %copy-done.8, bf16[1376,256]{1,0:T(8,128)(2,1)S(1)} %pad_maximum_fusion.13.grad_ref), custom_call_target="tpu_custom_call" | custom-call | flops 9694085120 | bytes 3522560 | tf_op jit(solution)/shard_map/attend_back/pallas_call | solution.py:165
  362.0 12.4 %attend_back.9 = bf16[1376,384]{1,0:T(8,128)(2,1)S(1)} custom-call(bf16[1376,768]{1,0:T(8,128)(2,1)} %copy-done.1, f32[1376,1]{1,0:T(8,128)S(1)} %copy.53.bias_ref, f32[1376,256]{1,0:T(8,128)S(1)} %get-tuple-element.70.log_ref, bf16[1376,256]{1,0:T(8,128)(2,1)S(1)} %copy-done.6, bf16[1376,256]{1,0:T(8,128)(2,1)S(1)} %pad_maximum_fusion.12.grad_ref), custom_call_target="tpu_custom_call" | custom-call | flops 9694085120 | bytes 3522560 | tf_op jit(solution)/shard_map/attend_back/pallas_call | solution.py:165
  376.8 12.6 %attend_back.7 = bf16[1376,384]{1,0:T(8,128)(2,1)S(1)} custom-call(bf16[1376,768]{1,0:T(8,128)(2,1)} %copy-done.2, f32[1376,1]{1,0:T(8,128)S(1)} %copy.54.bias_ref, f32[1376,256]{1,0:T(8,128)S(1)} %copy-done.19, bf16[1376,256]{1,0:T(8,128)(2,1)S(1)} %copy-done.8, bf16[1376,256]{1,0:T(8,128)(2,1)S(1)} %pad_maximum_fusion.13.grad_ref), custom_call_target="tpu_custom_call" | custom-call | flops 9694085120 | bytes 3522560 | tf_op jit(solution)/shard_map/attend_back/pallas_call | solution.py:165
  389.5 12.7 %attend_back.8 = bf16[1376,384]{1,0:T(8,128)(2,1)S(1)} custom-call(bf16[1376,768]{1,0:T(8,128)(2,1)} %copy-done, f32[1376,1]{1,0:T(8,128)S(1)} %copy-done.10, f32[1376,256]{1,0:T(8,128)S(1)} %copy-done.14, bf16[1376,256]{1,0:T(8,128)(2,1)S(1)} %copy-done.4, bf16[1376,256]{1,0:T(8,128)(2,1)S(1)} %pad_maximum_fusion.14.grad_ref), custom_call_target="tpu_custom_call" | custom-call | flops 9694085120 | bytes 3522560 | tf_op jit(solution)/shard_map/attend_back/pallas_call | solution.py:165
  408.4 12.4 %attend_back.6 = bf16[1376,384]{1,0:T(8,128)(2,1)S(1)} custom-call(bf16[1376,768]{1,0:T(8,128)(2,1)} %copy-done.1, f32[1376,1]{1,0:T(8,128)S(1)} %copy-done.12, f32[1376,256]{1,0:T(8,128)S(1)} %copy-done.17, bf16[1376,256]{1,0:T(8,128)(2,1)S(1)} %copy-done.6, bf16[1376,256]{1,0:T(8,128)(2,1)S(1)} %pad_maximum_fusion.12.grad_ref), custom_call_target="tpu_custom_call" | custom-call | flops 9694085120 | bytes 3522560 | tf_op jit(solution)/shard_map/attend_back/pallas_call | solution.py:165
  424.5 5.8 collective-permute-done.32
  434.8 7.0 collective-permute-done.26
  441.8 4.3 collective-permute-done.28
  457.9 12.7 %attend_back.11 = bf16[1376,384]{1,0:T(8,128)(2,1)S(1)} custom-call(bf16[1376,768]{1,0:T(8,128)(2,1)} %copy-done, f32[1376,1]{1,0:T(8,128)S(1)} %copy-done.10, f32[1376,256]{1,0:T(8,128)S(1)} %copy-done.15, bf16[1376,256]{1,0:T(8,128)(2,1)S(1)} %copy-done.4, bf16[1376,256]{1,0:T(8,128)(2,1)S(1)} %pad_maximum_fusion.14.grad_ref), custom_call_target="tpu_custom_call" | custom-call | flops 9694085120 | bytes 3522560 | tf_op jit(solution)/shard_map/attend_back/pallas_call | solution.py:165
  476.4 3.9 fusion.12
  485.2 16.5 %multiply_reduce_fusion = (f32[1024]{0:T(1024)}, bf16[1032,1024]{1,0:T(8,128)(2,1)}) fusion(bf16[3,344,1024]{2,1,0:T(8,128)(2,1)S(1)} %copy-done.29, f32[1032]{0:T(1024)S(1)} %reshape.428, f32[1032,1024]{1,0:T(8,128)S(1)} %bitcast.142, f32[1024]{0:T(1024)S(1)} %bitcast.169, f32[1024]{0:T(1024)S(1)} %bitcast.189, bf16[1032,4096]{1,0:T(8,128)(2,1)} %copy-done.131, ...), kind=kOutput, calls=%fused_computation.20 | convolution fusion | flops 8666553344 | bytes 25313312 | tf_op jit(solution)/shard_map/dot_general | solution.py:439
  511.0 5.3 fusion.53
  532.3 8.2 %collective-permute-start.70 = (f32[14,1024]{1,0:T(8,128)S(1)}, f32[14,1024]{1,0:T(8,128)S(1)}, u32[]{:S(2)}, u32[]{:S(2)}) collective-permute-start(f32[14,1024]{1,0:T(8,128)S(1)} %add.600), channel_id=1, source_target_pairs={{0,2},{2,0},{1,3},{3,1},{4,6},{6,4},{5,7},{7,5},{8,10},{10,8},{9,1... | collective-permute-start | bytes 172040 | tf_op jit(solution)/shard_map/ppermute | solution.py:199
  542.3 54.1 %collective-permute-done.70 = f32[14,1024]{1,0:T(8,128)S(1)} collective-permute-done((f32[14,1024]{1,0:T(8,128)S(1)}, f32[14,1024]{1,0:T(8,128)S(1)}, u32[]{:S(2)}, u32[]{:S(2)}) %collective-permute-start.70) | collective-permute-done | bytes 57376 | tf_op jit(solution)/shard_map/ppermute | solution.py:199
  597.9 3.7 fusion.5
  606.4 7.3 collective-permute-done.61
  618.0 8.0 %collective-permute-done.62 = bf16[128,1536]{1,0:T(8,128)(2,1)S(1)} collective-permute-done((bf16[128,1536]{1,0:T(8,128)(2,1)S(1)}, bf16[128,1536]{1,0:T(8,128)(2,1)S(1)}, u32[]{:S(2)}, u32[]{:S(2)}) %collective-permute-start.62) | collective-permute-done | bytes 393248 | tf_op jit(solution)/shard_map/ppermute | solution.py:261
  626.1 5.9 collective-permute-done.55
  633.9 3.7 collective-permute-done.63
  639.2 3.6 collective-permute-done.56
  644.7 3.9 collective-permute-done.64
  648.7 6.9 collective-permute-done.57
  657.4 14.6 %collective-permute-done.58 = bf16[64,2560]{1,0:T(8,128)(2,1)S(1)} collective-permute-done((bf16[64,2560]{1,0:T(8,128)(2,1)S(1)}, bf16[64,2560]{1,0:T(8,128)(2,1)S(1)}, u32[]{:S(2)}, u32[]{:S(2)}) %collective-permute-start.58) | collective-permute-done | bytes 327712 | tf_op jit(solution)/shard_map/ppermute | solution.py:199
  672.4 18.2 %collective-permute-done.59 = bf16[64,2560]{1,0:T(8,128)(2,1)S(1)} collective-permute-done((bf16[64,2560]{1,0:T(8,128)(2,1)S(1)}, bf16[64,2560]{1,0:T(8,128)(2,1)S(1)}, u32[]{:S(2)}, u32[]{:S(2)}) %collective-permute-start.59) | collective-permute-done | bytes 327712 | tf_op jit(solution)/shard_map/ppermute | solution.py:199
  697.2 62.7 %all-reduce.3.cloned.1.call-done = (bf16[128,4096]{1,0:T(8,128)(2,1)}, bf16[512,1024]{1,0:T(8,128)(2,1)}) async-done(((bf16[128,4096]{1,0:T(8,128)(2,1)}, bf16[512,1024]{1,0:T(8,128)(2,1)}), (bf16[128,4096]{1,0:T(8,128)(2,1)}, bf16[512,1024]{1,0:T(8,128)(2,1)})) %all-reduce.3.cloned.1.call-update) | async-done | bytes 2097168 | tf_op jit(solution)/shard_map/psum | solution.py:428
  (609 shorter events, 185.9 us)
Async XLA Ops:
  7.2 52.7 %all-gather.7.cloned.1.call-start = ((), (), s32[]{:S(2)}) async-start(), calls=%async_computation.2 | async-start | bytes 7077888 | tf_op jit(solution)/shard_map/all_gather | solution.py:348
  9.7 184.7 %all-gather.9.cloned.1.call-start = ((), (), s32[]{:S(2)}) async-start(), calls=%async_computation.3 | async-start | bytes 2359296 | tf_op jit(solution)/shard_map/all_gather | solution.py:349
  10.5 199.2 %all-gather.11.cloned.1.call-start = ((), (), s32[]{:S(2)}) async-start(), calls=%async_computation.4 | async-start | bytes 9437184 | tf_op jit(solution)/shard_map/all_gather | solution.py:350
  11.3 236.3 %all-gather.13.cloned.1.call-start = ((), (), s32[]{:S(2)}) async-start(), calls=%async_computation.5 | async-start | bytes 9437184 | tf_op jit(solution)/shard_map/all_gather | solution.py:351
  12.7 29.1 %collective-permute-start = (bf16[344,1024]{1,0:T(8,128)(2,1)}, bf16[344,1024]{1,0:T(8,128)(2,1)S(1)}, u32[]{:S(2)}, u32[]{:S(2)}) collective-permute-start(bf16[344,1024]{1,0:T(8,128)(2,1)} %get-tuple-element.218), channel_id=1, source_target_pairs={{2,4},{4,2},{3,5},{5,3},{10,12},{12,10},{11,13},{13,11},{18,20},{2... | collective-permute-start | bytes 2113544 | tf_op jit(solution)/shard_map/ppermute | solution.py:193
  13.4 28.4 %collective-permute-start.1 = (bf16[344,1024]{1,0:T(8,128)(2,1)}, bf16[344,1024]{1,0:T(8,128)(2,1)S(1)}, u32[]{:S(2)}, u32[]{:S(2)}) collective-permute-start(bf16[344,1024]{1,0:T(8,128)(2,1)} %get-tuple-element.219), channel_id=1, source_target_pairs={{2,4},{4,2},{3,5},{5,3},{10,12},{12,10},{11,13},{13,11},{18,20},{2... | collective-permute-start | bytes 2113544 | tf_op jit(solution)/shard_map/ppermute | solution.py:193
  14.1 27.7 %collective-permute-start.2 = (bf16[344,1024]{1,0:T(8,128)(2,1)}, bf16[344,1024]{1,0:T(8,128)(2,1)}, u32[]{:S(2)}, u32[]{:S(2)}) collective-permute-start(bf16[344,1024]{1,0:T(8,128)(2,1)} %get-tuple-element.217), channel_id=1, source_target_pairs={{2,4},{4,2},{3,5},{5,3},{10,12},{12,10},{11,13},{13,11},{18,20},{2... | collective-permute-start | bytes 2113544 | tf_op jit(solution)/shard_map/ppermute | solution.py:193
  15.9 22.8 %collective-permute-start.6 = (s32[6]{0:T(128)S(1)}, s32[6]{0:T(128)S(1)}, u32[]{:S(2)}, u32[]{:S(2)}) collective-permute-start(s32[6]{0:T(128)S(1)} %pad_add_fusion), channel_id=1, source_target_pairs={{2,4},{4,2},{3,5},{5,3},{10,12},{12,10},{11,13},{13,11},{18,20},{2... | collective-permute-start | bytes 80 | tf_op jit(solution)/shard_map/ppermute | solution.py:193
  16.6 655.6 %reduce-scatter.3.cloned.1.call-start = ((), (), s32[]{:S(2)}) async-start(), calls=%async_computation.6 | async-start | bytes 9437184 | tf_op jit(solution)/shard_map/reduce_scatter | solution.py:392
  65.7 26.1 %collective-permute-start.3 = (bf16[344,768]{1,0:T(8,128)(2,1)S(1)}, bf16[344,768]{1,0:T(8,128)(2,1)S(1)}, u32[]{:S(2)}, u32[]{:S(2)}) collective-permute-start(bf16[344,768]{1,0:T(8,128)(2,1)S(1)} %pad_maximum_fusion.15), channel_id=1, source_target_pairs={{0,1},{1,0},{4,5},{5,4},{2,3},{3,2},{6,7},{7,6},{8,9},{9,8},{12,13... | collective-permute-start | bytes 1585160 | tf_op jit(solution)/shard_map/ppermute | solution.py:199
  67.2 27.8 %collective-permute-start.4 = (bf16[344,768]{1,0:T(8,128)(2,1)S(1)}, bf16[344,768]{1,0:T(8,128)(2,1)S(1)}, u32[]{:S(2)}, u32[]{:S(2)}) collective-permute-start(bf16[344,768]{1,0:T(8,128)(2,1)S(1)} %pad_maximum_fusion.16), channel_id=1, source_target_pairs={{0,4},{1,5},{4,0},{5,1},{2,6},{3,7},{6,2},{7,3},{8,12},{9,13},{12,... | collective-permute-start | bytes 1585160 | tf_op jit(solution)/shard_map/ppermute | solution.py:199
  83.5 23.3 %collective-permute-start.5 = (bf16[344,768]{1,0:T(8,128)(2,1)S(1)}, bf16[344,768]{1,0:T(8,128)(2,1)S(1)}, u32[]{:S(2)}, u32[]{:S(2)}) collective-permute-start(bf16[344,768]{1,0:T(8,128)(2,1)S(1)} %pad_maximum_fusion.17), channel_id=1, source_target_pairs={{0,5},{1,4},{4,1},{5,0},{2,7},{3,6},{6,3},{7,2},{8,13},{9,12},{12,... | collective-permute-start | bytes 1585160 | tf_op jit(solution)/shard_map/ppermute | solution.py:199
  87.3 33.2 %collective-permute-start.10 = (bf16[344,768]{1,0:T(8,128)(2,1)S(1)}, bf16[344,768]{1,0:T(8,128)(2,1)S(1)}, u32[]{:S(2)}, u32[]{:S(2)}) collective-permute-start(bf16[344,768]{1,0:T(8,128)(2,1)S(1)} %pad_maximum_fusion.18), channel_id=1, source_target_pairs={{0,1},{1,0},{4,5},{5,4},{2,3},{3,2},{6,7},{7,6},{8,9},{9,8},{12,13... | collective-permute-start | bytes 1585160 | tf_op jit(solution)/shard_map/ppermute | solution.py:199
  88.1 32.5 %collective-permute-start.11 = (bf16[344,768]{1,0:T(8,128)(2,1)S(1)}, bf16[344,768]{1,0:T(8,128)(2,1)S(1)}, u32[]{:S(2)}, u32[]{:S(2)}) collective-permute-start(bf16[344,768]{1,0:T(8,128)(2,1)S(1)} %pad_maximum_fusion.19), channel_id=1, source_target_pairs={{0,4},{1,5},{4,0},{5,1},{2,6},{3,7},{6,2},{7,3},{8,12},{9,13},{12,... | collective-permute-start | bytes 1585160 | tf_op jit(solution)/shard_map/ppermute | solution.py:199
  91.8 37.7 %collective-permute-start.12 = (bf16[344,768]{1,0:T(8,128)(2,1)S(1)}, bf16[344,768]{1,0:T(8,128)(2,1)S(1)}, u32[]{:S(2)}, u32[]{:S(2)}) collective-permute-start(bf16[344,768]{1,0:T(8,128)(2,1)S(1)} %pad_maximum_fusion.20), channel_id=1, source_target_pairs={{0,5},{1,4},{4,1},{5,0},{2,7},{3,6},{6,3},{7,2},{8,13},{9,12},{12,... | collective-permute-start | bytes 1585160 | tf_op jit(solution)/shard_map/ppermute | solution.py:199
  95.0 47.5 %collective-permute-start.16 = (bf16[344,768]{1,0:T(8,128)(2,1)S(1)}, bf16[344,768]{1,0:T(8,128)(2,1)S(1)}, u32[]{:S(2)}, u32[]{:S(2)}) collective-permute-start(bf16[344,768]{1,0:T(8,128)(2,1)S(1)} %pad_maximum_fusion.21), channel_id=1, source_target_pairs={{0,1},{1,0},{4,5},{5,4},{2,3},{3,2},{6,7},{7,6},{8,9},{9,8},{12,13... | collective-permute-start | bytes 1585160 | tf_op jit(solution)/shard_map/ppermute | solution.py:199
  106.8 36.0 %collective-permute-start.17 = (bf16[344,768]{1,0:T(8,128)(2,1)S(1)}, bf16[344,768]{1,0:T(8,128)(2,1)S(1)}, u32[]{:S(2)}, u32[]{:S(2)}) collective-permute-start(bf16[344,768]{1,0:T(8,128)(2,1)S(1)} %pad_maximum_fusion.22), channel_id=1, source_target_pairs={{0,4},{1,5},{4,0},{5,1},{2,6},{3,7},{6,2},{7,3},{8,12},{9,13},{12,... | collective-permute-start | bytes 1585160 | tf_op jit(solution)/shard_map/ppermute | solution.py:199
  120.5 31.0 %collective-permute-start.18 = (bf16[344,768]{1,0:T(8,128)(2,1)S(1)}, bf16[344,768]{1,0:T(8,128)(2,1)S(1)}, u32[]{:S(2)}, u32[]{:S(2)}) collective-permute-start(bf16[344,768]{1,0:T(8,128)(2,1)S(1)} %pad_maximum_fusion.23), channel_id=1, source_target_pairs={{0,5},{1,4},{4,1},{5,0},{2,7},{3,6},{6,3},{7,2},{8,13},{9,12},{12,... | collective-permute-start | bytes 1585160 | tf_op jit(solution)/shard_map/ppermute | solution.py:199
  120.7 32.7 %collective-permute-start.7 = (bf16[344,256]{1,0:T(8,128)(2,1)}, bf16[344,256]{1,0:T(8,128)(2,1)S(1)}, u32[]{:S(2)}, u32[]{:S(2)}) collective-permute-start(bf16[344,256]{1,0:T(8,128)(2,1)} %get-tuple-element.282), channel_id=1, source_target_pairs={{0,1},{1,0},{4,5},{5,4},{2,3},{3,2},{6,7},{7,6},{8,9},{9,8},{12,13... | collective-permute-start | bytes 528392 | tf_op jit(solution)/shard_map/ppermute | solution.py:199
  129.5 23.9 %collective-permute-start.8 = (bf16[344,256]{1,0:T(8,128)(2,1)S(1)}, bf16[344,256]{1,0:T(8,128)(2,1)S(1)}, u32[]{:S(2)}, u32[]{:S(2)}) collective-permute-start(bf16[344,256]{1,0:T(8,128)(2,1)S(1)} %get-tuple-element.281), channel_id=1, source_target_pairs={{0,4},{1,5},{4,0},{5,1},{2,6},{3,7},{6,2},{7,3},{8,12},{9,13},{12,... | collective-permute-start | bytes 528392 | tf_op jit(solution)/shard_map/ppermute | solution.py:199
  177.4 26.0 %collective-permute-start.22 = (bf16[3,344,1024]{2,1,0:T(8,128)(2,1)}, bf16[3,344,1024]{2,1,0:T(8,128)(2,1)}, u32[]{:S(2)}, u32[]{:S(2)}) collective-permute-start(bf16[3,344,1024]{2,1,0:T(8,128)(2,1)} %param.14), channel_id=1, source_target_pairs={{2,4},{4,2},{3,5},{5,3},{10,12},{12,10},{11,13},{13,11},{18,20},{2... | collective-permute-start | bytes 6340616 | tf_op jit(solution)/shard_map/ppermute | solution.py:193
  282.9 389.3 %reduce-scatter.5.cloned.1.call-start = ((), (), s32[]{:S(2)}) async-start(), calls=%async_computation.7 | async-start | bytes 9437184 | tf_op jit(solution)/shard_map/reduce_scatter | solution.py:387
  310.7 34.1 %collective-permute-start.29 = (bf16[344,256]{1,0:T(8,128)(2,1)S(1)}, bf16[344,256]{1,0:T(8,128)(2,1)S(1)}, u32[]{:S(2)}, u32[]{:S(2)}) collective-permute-start(bf16[344,256]{1,0:T(8,128)(2,1)S(1)} %get-tuple-element.267), channel_id=1, source_target_pairs={{0,1},{1,0},{4,5},{5,4},{2,3},{3,2},{6,7},{7,6},{8,9},{9,8},{12,13... | collective-permute-start | bytes 528392 | tf_op jit(solution)/shard_map/ppermute | solution.py:199
  338.3 21.5 %collective-permute-start.23 = (bf16[344,256]{1,0:T(8,128)(2,1)S(1)}, bf16[344,256]{1,0:T(8,128)(2,1)S(1)}, u32[]{:S(2)}, u32[]{:S(2)}) collective-permute-start(bf16[344,256]{1,0:T(8,128)(2,1)S(1)} %get-tuple-element.271), channel_id=1, source_target_pairs={{0,1},{1,0},{4,5},{5,4},{2,3},{3,2},{6,7},{7,6},{8,9},{9,8},{12,13... | collective-permute-start | bytes 528392 | tf_op jit(solution)/shard_map/ppermute | solution.py:199
  339.4 21.5 %collective-permute-start.24 = (bf16[344,256]{1,0:T(8,128)(2,1)S(1)}, bf16[344,256]{1,0:T(8,128)(2,1)S(1)}, u32[]{:S(2)}, u32[]{:S(2)}) collective-permute-start(bf16[344,256]{1,0:T(8,128)(2,1)S(1)} %get-tuple-element.270), channel_id=1, source_target_pairs={{0,4},{1,5},{4,0},{5,1},{2,6},{3,7},{6,2},{7,3},{8,12},{9,13},{12,... | collective-permute-start | bytes 528392 | tf_op jit(solution)/shard_map/ppermute | solution.py:199
  345.7 28.8 %collective-permute-start.35 = (bf16[344,256]{1,0:T(8,128)(2,1)S(1)}, bf16[344,256]{1,0:T(8,128)(2,1)S(1)}, u32[]{:S(2)}, u32[]{:S(2)}) collective-permute-start(bf16[344,256]{1,0:T(8,128)(2,1)S(1)} %get-tuple-element.263), channel_id=1, source_target_pairs={{0,1},{1,0},{4,5},{5,4},{2,3},{3,2},{6,7},{7,6},{8,9},{9,8},{12,13... | collective-permute-start | bytes 528392 | tf_op jit(solution)/shard_map/ppermute | solution.py:199
  346.8 29.0 %collective-permute-start.36 = (bf16[344,256]{1,0:T(8,128)(2,1)S(1)}, bf16[344,256]{1,0:T(8,128)(2,1)S(1)}, u32[]{:S(2)}, u32[]{:S(2)}) collective-permute-start(bf16[344,256]{1,0:T(8,128)(2,1)S(1)} %get-tuple-element.262), channel_id=1, source_target_pairs={{0,4},{1,5},{4,0},{5,1},{2,6},{3,7},{6,2},{7,3},{8,12},{9,13},{12,... | collective-permute-start | bytes 528392 | tf_op jit(solution)/shard_map/ppermute | solution.py:199
  360.9 43.2 %collective-permute-start.44 = (bf16[344,384]{1,0:T(8,128)(2,1)S(1)}, bf16[344,384]{1,0:T(8,128)(2,1)S(1)}, u32[]{:S(2)}, u32[]{:S(2)}) collective-permute-start(bf16[344,384]{1,0:T(8,128)(2,1)S(1)} %get-tuple-element.242), channel_id=1, source_target_pairs={{0,1},{1,0},{4,5},{5,4},{2,3},{3,2},{6,7},{7,6},{8,9},{9,8},{12,13... | collective-permute-start | bytes 792584 | tf_op jit(solution)/shard_map/ppermute | solution.py:199
  361.9 43.3 %collective-permute-start.45 = (bf16[344,384]{1,0:T(8,128)(2,1)S(1)}, bf16[344,384]{1,0:T(8,128)(2,1)S(1)}, u32[]{:S(2)}, u32[]{:S(2)}) collective-permute-start(bf16[344,384]{1,0:T(8,128)(2,1)S(1)} %get-tuple-element.241), channel_id=1, source_target_pairs={{0,4},{1,5},{4,0},{5,1},{2,6},{3,7},{6,2},{7,3},{8,12},{9,13},{12,... | collective-permute-start | bytes 792584 | tf_op jit(solution)/shard_map/ppermute | solution.py:199
  374.5 31.7 %collective-permute-start.46 = (bf16[344,384]{1,0:T(8,128)(2,1)S(1)}, bf16[344,384]{1,0:T(8,128)(2,1)S(1)}, u32[]{:S(2)}, u32[]{:S(2)}) collective-permute-start(bf16[344,384]{1,0:T(8,128)(2,1)S(1)} %get-tuple-element.240), channel_id=1, source_target_pairs={{0,5},{1,4},{4,1},{5,0},{2,7},{3,6},{6,3},{7,2},{8,13},{9,12},{12,... | collective-permute-start | bytes 792584 | tf_op jit(solution)/shard_map/ppermute | solution.py:199
  375.7 30.5 %collective-permute-start.41 = (bf16[344,384]{1,0:T(8,128)(2,1)S(1)}, bf16[344,384]{1,0:T(8,128)(2,1)S(1)}, u32[]{:S(2)}, u32[]{:S(2)}) collective-permute-start(bf16[344,384]{1,0:T(8,128)(2,1)S(1)} %get-tuple-element.246), channel_id=1, source_target_pairs={{0,1},{1,0},{4,5},{5,4},{2,3},{3,2},{6,7},{7,6},{8,9},{9,8},{12,13... | collective-permute-start | bytes 792584 | tf_op jit(solution)/shard_map/ppermute | solution.py:199
  376.7 30.6 %collective-permute-start.42 = (bf16[344,384]{1,0:T(8,128)(2,1)S(1)}, bf16[344,384]{1,0:T(8,128)(2,1)S(1)}, u32[]{:S(2)}, u32[]{:S(2)}) collective-permute-start(bf16[344,384]{1,0:T(8,128)(2,1)S(1)} %get-tuple-element.245), channel_id=1, source_target_pairs={{0,4},{1,5},{4,0},{5,1},{2,6},{3,7},{6,2},{7,3},{8,12},{9,13},{12,... | collective-permute-start | bytes 792584 | tf_op jit(solution)/shard_map/ppermute | solution.py:199
  407.4 23.0 %collective-permute-start.32 = (bf16[344,384]{1,0:T(8,128)(2,1)S(1)}, bf16[344,384]{1,0:T(8,128)(2,1)S(1)}, u32[]{:S(2)}, u32[]{:S(2)}) collective-permute-start(bf16[344,384]{1,0:T(8,128)(2,1)S(1)} %get-tuple-element.254), channel_id=1, source_target_pairs={{0,1},{1,0},{4,5},{5,4},{2,3},{3,2},{6,7},{7,6},{8,9},{9,8},{12,13... | collective-permute-start | bytes 792584 | tf_op jit(solution)/shard_map/ppermute | solution.py:199
  423.1 18.7 %collective-permute-start.26 = (bf16[344,384]{1,0:T(8,128)(2,1)}, bf16[344,384]{1,0:T(8,128)(2,1)}, u32[]{:S(2)}, u32[]{:S(2)}) collective-permute-start(bf16[344,384]{1,0:T(8,128)(2,1)} %get-tuple-element.258), channel_id=1, source_target_pairs={{0,1},{1,0},{4,5},{5,4},{2,3},{3,2},{6,7},{7,6},{8,9},{9,8},{12,13... | collective-permute-start | bytes 792584 | tf_op jit(solution)/shard_map/ppermute | solution.py:199
  432.2 327.6 %all-reduce.3.cloned.1.call-start = ((), (), s32[]{:S(2)}) async-start(), calls=%async_computation.8 | async-start | bytes 4194304 | tf_op jit(solution)/shard_map/psum | solution.py:428
  472.3 29.9 %collective-permute-start.48 = (bf16[344,384]{1,0:T(8,128)(2,1)S(1)}, bf16[344,384]{1,0:T(8,128)(2,1)S(1)}, u32[]{:S(2)}, u32[]{:S(2)}) collective-permute-start(bf16[344,384]{1,0:T(8,128)(2,1)S(1)} %get-tuple-element.238), channel_id=1, source_target_pairs={{0,1},{1,0},{4,5},{5,4},{2,3},{3,2},{6,7},{7,6},{8,9},{9,8},{12,13... | collective-permute-start | bytes 792584 | tf_op jit(solution)/shard_map/ppermute | solution.py:199
  473.3 28.9 %collective-permute-start.49 = (bf16[344,384]{1,0:T(8,128)(2,1)S(1)}, bf16[344,384]{1,0:T(8,128)(2,1)S(1)}, u32[]{:S(2)}, u32[]{:S(2)}) collective-permute-start(bf16[344,384]{1,0:T(8,128)(2,1)S(1)} %get-tuple-element.237), channel_id=1, source_target_pairs={{0,4},{1,5},{4,0},{5,1},{2,6},{3,7},{6,2},{7,3},{8,12},{9,13},{12,... | collective-permute-start | bytes 792584 | tf_op jit(solution)/shard_map/ppermute | solution.py:199
  473.7 28.5 %collective-permute-start.50 = (bf16[344,384]{1,0:T(8,128)(2,1)S(1)}, bf16[344,384]{1,0:T(8,128)(2,1)S(1)}, u32[]{:S(2)}, u32[]{:S(2)}) collective-permute-start(bf16[344,384]{1,0:T(8,128)(2,1)S(1)} %get-tuple-element.236), channel_id=1, source_target_pairs={{0,5},{1,4},{4,1},{5,0},{2,7},{3,6},{6,3},{7,2},{8,13},{9,12},{12,... | collective-permute-start | bytes 792584 | tf_op jit(solution)/shard_map/ppermute | solution.py:199
  476.2 126.1 %collective-permute-start.54 = (bf16[512,2560]{1,0:T(8,128)(2,1)}, bf16[512,2560]{1,0:T(8,128)(2,1)}, u32[]{:S(2)}, u32[]{:S(2)}) collective-permute-start(bf16[512,2560]{1,0:T(8,128)(2,1)} %pad_maximum_fusion), channel_id=1, source_target_pairs={{0,4},{4,0},{1,5},{5,1},{2,6},{6,2},{3,7},{7,3},{8,12},{12,8},{9,1... | collective-permute-start | bytes 7864328 | tf_op jit(solution)/shard_map/ppermute | solution.py:199
  505.8 92.1 %collective-permute-start.60 = (bf16[512,1536]{1,0:T(8,128)(2,1)}, bf16[512,1536]{1,0:T(8,128)(2,1)}, u32[]{:S(2)}, u32[]{:S(2)}) collective-permute-start(bf16[512,1536]{1,0:T(8,128)(2,1)} %convolution_convert_fusion.3), channel_id=1, source_target_pairs={{0,4},{4,0},{1,5},{5,1},{2,6},{6,2},{3,7},{7,3},{8,12},{12,8},{9,1... | collective-permute-start | bytes 4718600 | tf_op jit(solution)/shard_map/ppermute | solution.py:199
  525.3 130.4 %collective-permute-start.47 = (bf16[3,344,1024]{2,1,0:T(8,128)(2,1)}, bf16[3,344,1024]{2,1,0:T(8,128)(2,1)S(1)}, u32[]{:S(2)}, u32[]{:S(2)}) collective-permute-start(bf16[3,344,1024]{2,1,0:T(8,128)(2,1)} %bitcast.153), channel_id=1, source_target_pairs={{2,4},{4,2},{3,5},{5,3},{10,12},{12,10},{11,13},{13,11},{18,20},{2... | collective-permute-start | bytes 6340616 | tf_op jit(solution)/shard_map/ppermute | solution.py:193
  526.1 89.9 %collective-permute-start.51 = (bf16[344,1024]{1,0:T(8,128)(2,1)}, bf16[344,1024]{1,0:T(8,128)(2,1)S(1)}, u32[]{:S(2)}, u32[]{:S(2)}) collective-permute-start(bf16[344,1024]{1,0:T(8,128)(2,1)} %get-tuple-element.184), channel_id=1, source_target_pairs={{2,4},{4,2},{3,5},{5,3},{10,12},{12,10},{11,13},{13,11},{18,20},{2... | collective-permute-start | bytes 2113544 | tf_op jit(solution)/shard_map/ppermute | solution.py:193
  532.3 64.1 %collective-permute-start.70 = (f32[14,1024]{1,0:T(8,128)S(1)}, f32[14,1024]{1,0:T(8,128)S(1)}, u32[]{:S(2)}, u32[]{:S(2)}) collective-permute-start(f32[14,1024]{1,0:T(8,128)S(1)} %add.600), channel_id=1, source_target_pairs={{0,2},{2,0},{1,3},{3,1},{4,6},{6,4},{5,7},{7,5},{8,10},{10,8},{9,1... | collective-permute-start | bytes 172040 | tf_op jit(solution)/shard_map/ppermute | solution.py:199
  596.4 37.4 %collective-permute-start.52 = (bf16[344,1024]{1,0:T(8,128)(2,1)S(1)}, bf16[344,1024]{1,0:T(8,128)(2,1)S(1)}, u32[]{:S(2)}, u32[]{:S(2)}) collective-permute-start(bf16[344,1024]{1,0:T(8,128)(2,1)S(1)} %fusion.52), channel_id=1, source_target_pairs={{2,4},{4,2},{3,5},{5,3},{10,12},{12,10},{11,13},{13,11},{18,20},{2... | collective-permute-start | bytes 2113544 | tf_op jit(solution)/shard_map/ppermute | solution.py:193
  605.6 26.4 %collective-permute-start.55 = (bf16[2,128,2560]{2,1,0:T(8,128)(2,1)S(1)}, bf16[2,128,2560]{2,1,0:T(8,128)(2,1)S(1)}, u32[]{:S(2)}, u32[]{:S(2)}) collective-permute-start(bf16[2,128,2560]{2,1,0:T(8,128)(2,1)S(1)} %bitcast.155), channel_id=1, source_target_pairs={{0,8},{4,20},{8,0},{12,28},{16,24},{20,4},{24,16},{28,12},{1,9},{5... | collective-permute-start | bytes 3932168 | tf_op jit(solution)/shard_map/ppermute | solution.py:259
  616.0 27.0 %collective-permute-start.53 = (bf16[344,1024]{1,0:T(8,128)(2,1)S(1)}, bf16[344,1024]{1,0:T(8,128)(2,1)S(1)}, u32[]{:S(2)}, u32[]{:S(2)}) collective-permute-start(bf16[344,1024]{1,0:T(8,128)(2,1)S(1)} %get-tuple-element.185), channel_id=1, source_target_pairs={{2,4},{4,2},{3,5},{5,3},{10,12},{12,10},{11,13},{13,11},{18,20},{2... | collective-permute-start | bytes 2113544 | tf_op jit(solution)/shard_map/ppermute | solution.py:193
  648.7 23.6 %collective-permute-start.65 = (bf16[64,1536]{1,0:T(8,128)(2,1)S(1)}, bf16[64,1536]{1,0:T(8,128)(2,1)S(1)}, u32[]{:S(2)}, u32[]{:S(2)}) collective-permute-start(bf16[64,1536]{1,0:T(8,128)(2,1)S(1)} %add.590), channel_id=1, source_target_pairs={{0,1},{1,0},{2,3},{3,2},{4,5},{5,4},{6,7},{7,6},{8,9},{9,8},{10,11... | collective-permute-start | bytes 589832 | tf_op jit(solution)/shard_map/ppermute | solution.py:199
  672.1 18.5 %collective-permute-start.59 = (bf16[64,2560]{1,0:T(8,128)(2,1)S(1)}, bf16[64,2560]{1,0:T(8,128)(2,1)S(1)}, u32[]{:S(2)}, u32[]{:S(2)}) collective-permute-start(bf16[64,2560]{1,0:T(8,128)(2,1)S(1)} %add.584), channel_id=1, source_target_pairs={{0,1},{1,0},{2,3},{3,2},{4,5},{5,4},{6,7},{7,6},{8,9},{9,8},{10,11... | collective-permute-start | bytes 983048 | tf_op jit(solution)/shard_map/ppermute | solution.py:199
  (170 other events, 2050.3 us)
Sparse Core Ops, SparseCore 0:
  10.5 49.4 all-gather.6
  61.8 27.9 all-gather.8
  91.7 54.4 all-gather.10
  147.9 54.3 all-gather.12
  283.0 98.2 reduce-scatter.2
  432.3 73.2 reduce-scatter.4
  672.4 87.4 all-reduce.2

commit v2 on v1

--- a/solution.py
+++ b/solution.py
@@ -424,9 +424,8 @@
         grad_parts.append(grad_slots)
     grad_parts[-1] = laid(grad_parts[-1])
     grad_w_qkv.append(products(rows_one, grad_parts[-1]))
-    grad_w_down, grad_w_up = (
-        grad.astype(jnp.float32) for grad in lax.psum((grad_w_down, grad_w_up), SEQ)
-    )
+    grad_w_up = summed_seq(grad_w_up)
+    grad_w_down = summed_seq(grad_w_down)
     grad_w_qkv[0] = [
         jnp.concatenate(both, axis=1) for both in zip(grad_w_qkv[0], grad_w_out, strict=True)
     ]

time: 782 us -> 785 us (level)
  waiting for transfers between devices: 266 us -> 246 us
  starting transfers between devices: 110 us -> 124 us
  other arithmetic: 50.6 us -> 58.5 us
    psum x1 -> x0, waiting for transfers between devices: 62.7 us -> none  [body(): lax.psum((grad_w_down, grad_w_up), SEQ)]
    ppermute x58 -> x64, waiting for transfers between devices: 167 us -> 209 us  [swapped(): return lax.ppermute(values, axis, [(n, n ^ bit) for n in range(count)])]
    ppermute x58 -> x64, starting transfers between devices: 95.7 us -> 110 us  [swapped(): return lax.ppermute(values, axis, [(n, n ^ bit) for n in range(count)])]
    unnamed x282 -> x292, local copies, waits for them, and re-layouts: 20.5 us -> 22.3 us
  transfers between devices with their start and end apart: 78 -> 83, of which waited for: 26 -> 30; matrix products, arithmetic and copies ran while one was open for 25% -> 26% of each run, Pallas kernels for 14% -> 14%
where the time goes in v2:
time: 785 us; the launch traced here: 775 us
  waiting for transfers between devices  246 us (31%)
  matrix products  155 us (20%)
  starting transfers between devices  124 us (16%)
  Pallas kernels  107 us (14%)
  other arithmetic  58.5 us (7%)
  local copies, waits for them, and re-layouts  47.7 us (6%)
  blocking collectives  19.4 us (2%)
  between operations  17.3 us (2%)
    ppermute x64, waiting for transfers between devices, swapped(): return lax.ppermute(values, axis, [(n, n ^ bit) for n in range(count)])  209 us
    ppermute x64, starting transfers between devices, swapped(): return lax.ppermute(values, axis, [(n, n ^ bit) for n in range(count)])  110 us
    pallas_call x6, Pallas kernels, attend_back(): pl.pallas_call(attend_back_kernel, grid=(1,), in_specs=[pl.BlockSpec((seq...  75.5 us
    dot_general x8, matrix products, product(): lax.dot_general(left, right, (((0,), (0,)), ((), ())), preferred_element_...  49.3 us
    pallas_call x3, Pallas kernels, attend(): pl.pallas_call(attend_kernel, out_shape=(jax.ShapeDtypeStruct((seq_len, w...  31.9 us
    unnamed x292, local copies, waits for them, and re-layouts  22.3 us
    dot_general x1, matrix products, body(): jnp.dot(normed_two, up_full, preferred_element_type=jnp.float32) + up_bias_f  21.3 us
    all_gather x1, blocking collectives, body(): small = lax.all_gather(small, IMG, axis=0, tiled=False).astype(jnp.float32)  19.4 us
  transfers between devices with their start and end apart: 83, of which 30 were waited for; matrix products, arithmetic and copies ran while one was open for 26% of the time, Pallas kernels for 14%

profile of v2, /device:TPU:0, one launch (start us, length us, event | category | flops | bytes accessed | tf_op | source)
XLA Modules:
  0.0 774.7 jit_solution(12351617217940257521)
XLA Ops:
  16.8 19.4 %all-gather.1 = bf16[8,14,128]{2,1,0:T(8,128)(2,1)S(1)} all-gather(bf16[1,14,128]{2,1,0:T(8,128)(2,1)S(1)} %bitcast.179), channel_id=2, replica_groups=mesh['chip'=4,'core'=2,'high'=2,'low'=2] {'chip','core'}, dimensions={0}, use_global_device_ids=true | all-gather | bytes 32256 | tf_op jit(solution)/shard_map/all_gather | solution.py:344
  51.9 8.0 %all-gather.7.cloned.1.call-done = bf16[1024,3072]{0,1:T(8,128)(2,1)} async-done(((bf16[128,3072]{0,1:T(8,128)(2,1)}), bf16[1024,3072]{0,1:T(8,128)(2,1)}) %all-gather.7.cloned.1.call-update) | async-done | bytes 6291472 | tf_op jit(solution)/shard_map/all_gather | solution.py:348
  59.9 5.4 add_convert_fusion.3
  67.4 19.0 %collective-permute-start.4 = (bf16[344,768]{1,0:T(8,128)(2,1)S(1)}, bf16[344,768]{1,0:T(8,128)(2,1)S(1)}, u32[]{:S(2)}, u32[]{:S(2)}) collective-permute-start(bf16[344,768]{1,0:T(8,128)(2,1)S(1)} %pad_maximum_fusion.16), channel_id=1, source_target_pairs={{0,4},{1,5},{4,0},{5,1},{2,6},{3,7},{6,2},{7,3},{8,12},{9,13},{12,... | collective-permute-start | bytes 1585160 | tf_op jit(solution)/shard_map/ppermute | solution.py:199
  99.9 9.9 %collective-permute-done.5 = bf16[344,768]{1,0:T(8,128)(2,1)S(1)} collective-permute-done((bf16[344,768]{1,0:T(8,128)(2,1)S(1)}, bf16[344,768]{1,0:T(8,128)(2,1)S(1)}, u32[]{:S(2)}, u32[]{:S(2)}) %collective-permute-start.5) | collective-permute-done | bytes 528416 | tf_op jit(solution)/shard_map/ppermute | solution.py:199
  111.5 10.6 %attend.3 = (bf16[1376,256]{1,0:T(8,128)(2,1)S(1)}, f32[1376,256]{1,0:T(8,128)S(1)}) custom-call(bf16[1376,768]{1,0:T(8,128)(2,1)S(1)} %pad_maximum_fusion.2.qkv_ref, f32[1376,1]{1,0:T(8,128)S(1)} %copy.53.bias_ref), custom_call_target="tpu_custom_call" | custom-call | flops 7755268096 | bytes 4931584 | tf_op jit(solution)/shard_map/attend/pallas_call | solution.py:146
  125.5 6.8 collective-permute-done.12
  134.5 10.6 %attend.4 = (bf16[1376,256]{1,0:T(8,128)(2,1)S(1)}, f32[1376,256]{1,0:T(8,128)S(1)}) custom-call(bf16[1376,768]{1,0:T(8,128)(2,1)S(1)} %pad_maximum_fusion.3.qkv_ref, f32[1376,1]{1,0:T(8,128)S(1)} %copy.54.bias_ref), custom_call_target="tpu_custom_call" | custom-call | flops 7755268096 | bytes 4931584 | tf_op jit(solution)/shard_map/attend/pallas_call | solution.py:146
  145.6 8.9 %collective-permute-done.18 = bf16[344,768]{1,0:T(8,128)(2,1)S(1)} collective-permute-done((bf16[344,768]{1,0:T(8,128)(2,1)S(1)}, bf16[344,768]{1,0:T(8,128)(2,1)S(1)}, u32[]{:S(2)}, u32[]{:S(2)}) %collective-permute-start.18) | collective-permute-done | bytes 528416 | tf_op jit(solution)/shard_map/ppermute | solution.py:199
  159.1 10.6 %attend.5 = (bf16[1376,256]{1,0:T(8,128)(2,1)S(1)}, f32[1376,256]{1,0:T(8,128)S(1)}) custom-call(bf16[1376,768]{1,0:T(8,128)(2,1)S(1)} %pad_maximum_fusion.4.qkv_ref, f32[1376,1]{1,0:T(8,128)S(1)} %copy.55.bias_ref), custom_call_target="tpu_custom_call" | custom-call | flops 7755268096 | bytes 4931584 | tf_op jit(solution)/shard_map/attend/pallas_call | solution.py:146
  171.4 4.6 collective-permute-done.15
  182.5 5.0 collective-permute-start.21
  187.6 6.5 collective-permute-done.21
  197.6 4.8 convolution_add_fusion.2
  212.8 21.3 %fusion.3 = (f32[1032,4096]{1,0:T(8,128)}, bf16[1032,4096]{1,0:T(8,128)(2,1)S(1)}) fusion(f32[4096]{0:T(1024)S(1)} %bitcast.180, bf16[1024,4096]{1,0:T(8,128)(2,1)} %all-gather.11.cloned.1.call-done, f32[1032,1024]{1,0:T(8,128)} %copy-done.20, f32[1024]{0:T(1024)S(1)} %bitcast.190, f32[1024]{0:T(1024)S(1)} %bitcast.170, f32[1032]{0:T(1024)S(1)} %fusion.79, ...), kind=kOutput, calls=%fused_computation.6 | convolution fusion | flops 8708825088 | bytes 38010944 | tf_op jit(solution)/shard_map/dot_general | solution.py:380
  237.5 13.1 %convolution_convert_fusion = bf16[4096,1024]{1,0:T(8,128)(2,1)} fusion(bf16[1032,4096]{1,0:T(8,128)(2,1)S(1)} %get-tuple-element.87, bf16[1032,1024]{1,0:T(8,128)(2,1)S(1)} %copy-done.50), kind=kOutput, calls=%fused_computation.11 | convolution fusion | flops 8661237760 | bytes 18956288 | tf_op jit(solution)/shard_map/dot_general | solution.py:241
  250.6 17.3 %convert_reduce_fusion = (f32[4096]{0:T(1024)}, bf16[1032,4096]{1,0:T(8,128)(2,1)}) fusion(f32[1032,4096]{1,0:T(8,128)} %get-tuple-element.66, bf16[1032,1024]{1,0:T(8,128)(2,1)} %multiply_convert_fusion.4, bf16[4096,1024]{1,0:T(8,128)(2,1)} %all-gather.13.cloned.1.call-done), kind=kOutput, calls=%fused_computation.7 | convolution fusion | flops 8673947648 | bytes 35880960 | tf_op jit(solution)/shard_map/dot_general | solution.py:388
  267.9 18.4 %convolution_convert_fusion.1 = bf16[1024,4096]{1,0:T(8,128)(2,1)} fusion(bf16[1032,4096]{1,0:T(8,128)(2,1)} %get-tuple-element.67, f32[1032,1024]{1,0:T(8,128)} %copy-done.20, f32[1024]{0:T(1024)S(1)} %bitcast.191, f32[1024]{0:T(1024)S(1)} %bitcast.171, f32[1032]{0:T(1024)S(1)} %fusion.79, f32[1032]{0:T(1024)S(1)} %broadcast_multiply_fusion), kind=kOutput, calls=%fused_computation.12 | convolution fusion | flops 8666521600 | bytes 21086272 | tf_op jit(solution)/shard_map/dot_general | solution.py:241
  286.4 16.1 %multiply_reduce_fusion.2 = (f32[1024]{0:T(1024)S(1)}, f32[1032]{0:T(1024)S(1)}, f32[1024]{0:T(1024)S(1)}, f32[1032,1024]{1,0:T(8,128)S(1)}) fusion(f32[1032,1024]{1,0:T(8,128)} %copy-done.20, f32[1032]{0:T(1024)S(1)} %fusion.79, f32[1032]{0:T(1024)S(1)} %broadcast_multiply_fusion, f32[1024]{0:T(1024)S(1)} %bitcast.172, ...), kind=kOutput, calls=%fused_computation.25 | convolution fusion | flops 8665494528 | bytes 25321568 | tf_op jit(solution)/shard_map/dot_general | solution.py:393
  313.5 23.5 %collective-permute-start.29 = (bf16[344,256]{1,0:T(8,128)(2,1)S(1)}, bf16[344,256]{1,0:T(8,128)(2,1)S(1)}, u32[]{:S(2)}, u32[]{:S(2)}) collective-permute-start(bf16[344,256]{1,0:T(8,128)(2,1)S(1)} %get-tuple-element.269), channel_id=1, source_target_pairs={{0,1},{1,0},{4,5},{5,4},{2,3},{3,2},{6,7},{7,6},{8,9},{9,8},{12,13... | collective-permute-start | bytes 528392 | tf_op jit(solution)/shard_map/ppermute | solution.py:199
  337.0 4.1 collective-permute-start.30
  350.4 12.6 %attend_back.10 = bf16[1376,384]{1,0:T(8,128)(2,1)S(1)} custom-call(bf16[1376,768]{1,0:T(8,128)(2,1)} %copy-done.2, f32[1376,1]{1,0:T(8,128)S(1)} %copy.54.bias_ref, f32[1376,256]{1,0:T(8,128)S(1)} %copy-done.19, bf16[1376,256]{1,0:T(8,128)(2,1)S(1)} %copy-done.8, bf16[1376,256]{1,0:T(8,128)(2,1)S(1)} %pad_maximum_fusion.13.grad_ref), custom_call_target="tpu_custom_call" | custom-call | flops 9694085120 | bytes 3522560 | tf_op jit(solution)/shard_map/attend_back/pallas_call | solution.py:165
  365.3 12.7 %attend_back.9 = bf16[1376,384]{1,0:T(8,128)(2,1)S(1)} custom-call(bf16[1376,768]{1,0:T(8,128)(2,1)} %copy-done.1, f32[1376,1]{1,0:T(8,128)S(1)} %copy.53.bias_ref, f32[1376,256]{1,0:T(8,128)S(1)} %get-tuple-element.70.log_ref, bf16[1376,256]{1,0:T(8,128)(2,1)S(1)} %copy-done.6, bf16[1376,256]{1,0:T(8,128)(2,1)S(1)} %pad_maximum_fusion.12.grad_ref), custom_call_target="tpu_custom_call" | custom-call | flops 9694085120 | bytes 3522560 | tf_op jit(solution)/shard_map/attend_back/pallas_call | solution.py:165
  381.1 12.6 %attend_back.7 = bf16[1376,384]{1,0:T(8,128)(2,1)S(1)} custom-call(bf16[1376,768]{1,0:T(8,128)(2,1)} %copy-done.2, f32[1376,1]{1,0:T(8,128)S(1)} %copy.54.bias_ref, f32[1376,256]{1,0:T(8,128)S(1)} %copy-done.19, bf16[1376,256]{1,0:T(8,128)(2,1)S(1)} %copy-done.8, bf16[1376,256]{1,0:T(8,128)(2,1)S(1)} %pad_maximum_fusion.13.grad_ref), custom_call_target="tpu_custom_call" | custom-call | flops 9694085120 | bytes 3522560 | tf_op jit(solution)/shard_map/attend_back/pallas_call | solution.py:165
  393.7 12.5 %attend_back.8 = bf16[1376,384]{1,0:T(8,128)(2,1)S(1)} custom-call(bf16[1376,768]{1,0:T(8,128)(2,1)} %copy-done, f32[1376,1]{1,0:T(8,128)S(1)} %copy-done.10, f32[1376,256]{1,0:T(8,128)S(1)} %copy-done.14, bf16[1376,256]{1,0:T(8,128)(2,1)S(1)} %copy-done.4, bf16[1376,256]{1,0:T(8,128)(2,1)S(1)} %pad_maximum_fusion.14.grad_ref), custom_call_target="tpu_custom_call" | custom-call | flops 9694085120 | bytes 3522560 | tf_op jit(solution)/shard_map/attend_back/pallas_call | solution.py:165
  411.6 12.7 %attend_back.6 = bf16[1376,384]{1,0:T(8,128)(2,1)S(1)} custom-call(bf16[1376,768]{1,0:T(8,128)(2,1)} %copy-done.1, f32[1376,1]{1,0:T(8,128)S(1)} %copy-done.12, f32[1376,256]{1,0:T(8,128)S(1)} %copy-done.17, bf16[1376,256]{1,0:T(8,128)(2,1)S(1)} %copy-done.6, bf16[1376,256]{1,0:T(8,128)(2,1)S(1)} %pad_maximum_fusion.12.grad_ref), custom_call_target="tpu_custom_call" | custom-call | flops 9694085120 | bytes 3522560 | tf_op jit(solution)/shard_map/attend_back/pallas_call | solution.py:165
  427.7 5.8 collective-permute-done.32
  437.9 7.0 collective-permute-done.26
  445.0 4.3 collective-permute-done.28
  461.1 12.4 %attend_back.11 = bf16[1376,384]{1,0:T(8,128)(2,1)S(1)} custom-call(bf16[1376,768]{1,0:T(8,128)(2,1)} %copy-done, f32[1376,1]{1,0:T(8,128)S(1)} %copy-done.10, f32[1376,256]{1,0:T(8,128)S(1)} %copy-done.15, bf16[1376,256]{1,0:T(8,128)(2,1)S(1)} %copy-done.4, bf16[1376,256]{1,0:T(8,128)(2,1)S(1)} %pad_maximum_fusion.14.grad_ref), custom_call_target="tpu_custom_call" | custom-call | flops 9694085120 | bytes 3522560 | tf_op jit(solution)/shard_map/attend_back/pallas_call | solution.py:165
  487.3 15.7 %multiply_reduce_fusion = (f32[1024]{0:T(1024)S(1)}, bf16[1032,1024]{1,0:T(8,128)(2,1)}) fusion(bf16[3,344,1024]{2,1,0:T(8,128)(2,1)S(1)} %copy-done.27, f32[1032]{0:T(1024)S(1)} %reshape.428, f32[1032,1024]{1,0:T(8,128)S(1)} %bitcast.142, f32[1024]{0:T(1024)S(1)} %bitcast.169, f32[1024]{0:T(1024)S(1)} %bitcast.189, bf16[1032,4096]{1,0:T(8,128)(2,1)} %copy-done.138, ...), kind=kOutput, calls=%fused_computation.20 | convolution fusion | flops 8666553344 | bytes 25313312 | tf_op jit(solution)/shard_map/dot_general | solution.py:438
  515.4 5.9 fusion.53
  538.1 7.8 %collective-permute-start.76 = (f32[14,1024]{1,0:T(8,128)S(1)}, f32[14,1024]{1,0:T(8,128)S(1)}, u32[]{:S(2)}, u32[]{:S(2)}) collective-permute-start(f32[14,1024]{1,0:T(8,128)S(1)} %add.622), channel_id=1, source_target_pairs={{0,2},{2,0},{1,3},{3,1},{4,6},{6,4},{5,7},{7,5},{8,10},{10,8},{9,1... | collective-permute-start | bytes 172040 | tf_op jit(solution)/shard_map/ppermute | solution.py:199
  548.4 53.4 %collective-permute-done.76 = f32[14,1024]{1,0:T(8,128)S(1)} collective-permute-done((f32[14,1024]{1,0:T(8,128)S(1)}, f32[14,1024]{1,0:T(8,128)S(1)}, u32[]{:S(2)}, u32[]{:S(2)}) %collective-permute-start.76) | collective-permute-done | bytes 57376 | tf_op jit(solution)/shard_map/ppermute | solution.py:199
  604.7 3.7 fusion.5
  612.4 8.2 %collective-permute-done.61 = bf16[2,128,1536]{2,1,0:T(8,128)(2,1)S(1)} collective-permute-done((bf16[2,128,1536]{2,1,0:T(8,128)(2,1)S(1)}, bf16[2,128,1536]{2,1,0:T(8,128)(2,1)S(1)}, u32[]{:S(2)}, u32[]{:S(2)}) %collective-permute-start.61) | collective-permute-done | bytes 786464 | tf_op jit(solution)/shard_map/ppermute | solution.py:259
  622.9 10.3 %collective-permute-done.62 = bf16[128,1536]{1,0:T(8,128)(2,1)S(1)} collective-permute-done((bf16[128,1536]{1,0:T(8,128)(2,1)S(1)}, bf16[128,1536]{1,0:T(8,128)(2,1)S(1)}, u32[]{:S(2)}, u32[]{:S(2)}) %collective-permute-start.62) | collective-permute-done | bytes 393248 | tf_op jit(solution)/shard_map/ppermute | solution.py:261
  633.3 9.1 %collective-permute-done.55 = bf16[2,128,2560]{2,1,0:T(8,128)(2,1)S(1)} collective-permute-done((bf16[2,128,2560]{2,1,0:T(8,128)(2,1)S(1)}, bf16[2,128,2560]{2,1,0:T(8,128)(2,1)S(1)}, u32[]{:S(2)}, u32[]{:S(2)}) %collective-permute-start.55) | collective-permute-done | bytes 1310752 | tf_op jit(solution)/shard_map/ppermute | solution.py:259
  645.9 7.5 collective-permute-start.64
  658.8 5.4 collective-permute-done.57
  664.3 4.2 collective-permute-start.58
  668.9 12.3 %collective-permute-done.58 = bf16[64,2560]{1,0:T(8,128)(2,1)S(1)} collective-permute-done((bf16[64,2560]{1,0:T(8,128)(2,1)S(1)}, bf16[64,2560]{1,0:T(8,128)(2,1)S(1)}, u32[]{:S(2)}, u32[]{:S(2)}) %collective-permute-start.58) | collective-permute-done | bytes 327712 | tf_op jit(solution)/shard_map/ppermute | solution.py:199
  686.6 5.5 collective-permute-done.59
  693.1 10.2 %collective-permute-done.69 = bf16[256,1024]{1,0:T(8,128)(2,1)} collective-permute-done((bf16[256,1024]{1,0:T(8,128)(2,1)}, bf16[256,1024]{1,0:T(8,128)(2,1)}, u32[]{:S(2)}, u32[]{:S(2)}) %collective-permute-start.69) | collective-permute-done | bytes 524320 | tf_op jit(solution)/shard_map/ppermute | solution.py:199
  704.7 15.1 %collective-permute-done.66 = bf16[64,4096]{1,0:T(8,128)(2,1)S(1)} collective-permute-done((bf16[64,4096]{1,0:T(8,128)(2,1)S(1)}, bf16[64,4096]{1,0:T(8,128)(2,1)S(1)}, u32[]{:S(2)}, u32[]{:S(2)}) %collective-permute-start.66) | collective-permute-done | bytes 524320 | tf_op jit(solution)/shard_map/ppermute | solution.py:199
  720.8 20.6 %collective-permute-done.70 = bf16[256,1024]{1,0:T(8,128)(2,1)S(1)} collective-permute-done((bf16[256,1024]{1,0:T(8,128)(2,1)S(1)}, bf16[256,1024]{1,0:T(8,128)(2,1)S(1)}, u32[]{:S(2)}, u32[]{:S(2)}) %collective-permute-start.70) | collective-permute-done | bytes 524320 | tf_op jit(solution)/shard_map/ppermute | solution.py:199
  745.0 4.1 collective-permute-done.67
  751.4 8.4 %collective-permute-done.71 = bf16[256,1024]{1,0:T(8,128)(2,1)} collective-permute-done((bf16[256,1024]{1,0:T(8,128)(2,1)}, bf16[256,1024]{1,0:T(8,128)(2,1)}, u32[]{:S(2)}, u32[]{:S(2)}) %collective-permute-start.71) | collective-permute-done | bytes 524320 | tf_op jit(solution)/shard_map/ppermute | solution.py:199
  (635 shorter events, 213.4 us)
Async XLA Ops:
  7.2 52.7 %all-gather.7.cloned.1.call-start = ((), (), s32[]{:S(2)}) async-start(), calls=%async_computation.2 | async-start | bytes 7077888 | tf_op jit(solution)/shard_map/all_gather | solution.py:348
  9.7 187.9 %all-gather.9.cloned.1.call-start = ((), (), s32[]{:S(2)}) async-start(), calls=%async_computation.3 | async-start | bytes 2359296 | tf_op jit(solution)/shard_map/all_gather | solution.py:349
  10.5 202.3 %all-gather.11.cloned.1.call-start = ((), (), s32[]{:S(2)}) async-start(), calls=%async_computation.4 | async-start | bytes 9437184 | tf_op jit(solution)/shard_map/all_gather | solution.py:350
  11.3 239.3 %all-gather.13.cloned.1.call-start = ((), (), s32[]{:S(2)}) async-start(), calls=%async_computation.5 | async-start | bytes 9437184 | tf_op jit(solution)/shard_map/all_gather | solution.py:351
  12.7 29.1 %collective-permute-start = (bf16[344,1024]{1,0:T(8,128)(2,1)}, bf16[344,1024]{1,0:T(8,128)(2,1)S(1)}, u32[]{:S(2)}, u32[]{:S(2)}) collective-permute-start(bf16[344,1024]{1,0:T(8,128)(2,1)} %get-tuple-element.216), channel_id=1, source_target_pairs={{2,4},{4,2},{3,5},{5,3},{10,12},{12,10},{11,13},{13,11},{18,20},{2... | collective-permute-start | bytes 2113544 | tf_op jit(solution)/shard_map/ppermute | solution.py:193
  13.4 28.4 %collective-permute-start.1 = (bf16[344,1024]{1,0:T(8,128)(2,1)}, bf16[344,1024]{1,0:T(8,128)(2,1)S(1)}, u32[]{:S(2)}, u32[]{:S(2)}) collective-permute-start(bf16[344,1024]{1,0:T(8,128)(2,1)} %get-tuple-element.217), channel_id=1, source_target_pairs={{2,4},{4,2},{3,5},{5,3},{10,12},{12,10},{11,13},{13,11},{18,20},{2... | collective-permute-start | bytes 2113544 | tf_op jit(solution)/shard_map/ppermute | solution.py:193
  14.1 29.4 %collective-permute-start.2 = (bf16[344,1024]{1,0:T(8,128)(2,1)}, bf16[344,1024]{1,0:T(8,128)(2,1)}, u32[]{:S(2)}, u32[]{:S(2)}) collective-permute-start(bf16[344,1024]{1,0:T(8,128)(2,1)} %get-tuple-element.215), channel_id=1, source_target_pairs={{2,4},{4,2},{3,5},{5,3},{10,12},{12,10},{11,13},{13,11},{18,20},{2... | collective-permute-start | bytes 2113544 | tf_op jit(solution)/shard_map/ppermute | solution.py:193
  15.9 22.8 %collective-permute-start.6 = (s32[6]{0:T(128)S(1)}, s32[6]{0:T(128)S(1)}, u32[]{:S(2)}, u32[]{:S(2)}) collective-permute-start(s32[6]{0:T(128)S(1)} %pad_add_fusion), channel_id=1, source_target_pairs={{2,4},{4,2},{3,5},{5,3},{10,12},{12,10},{11,13},{13,11},{18,20},{2... | collective-permute-start | bytes 80 | tf_op jit(solution)/shard_map/ppermute | solution.py:193
  16.6 664.8 %reduce-scatter.5.cloned.1.call-start = ((), (), s32[]{:S(2)}) async-start(), calls=%async_computation.7 | async-start | bytes 9437184 | tf_op jit(solution)/shard_map/reduce_scatter | solution.py:387
  65.8 30.3 %collective-permute-start.3 = (bf16[344,768]{1,0:T(8,128)(2,1)S(1)}, bf16[344,768]{1,0:T(8,128)(2,1)S(1)}, u32[]{:S(2)}, u32[]{:S(2)}) collective-permute-start(bf16[344,768]{1,0:T(8,128)(2,1)S(1)} %pad_maximum_fusion.15), channel_id=1, source_target_pairs={{0,1},{1,0},{4,5},{5,4},{2,3},{3,2},{6,7},{7,6},{8,9},{9,8},{12,13... | collective-permute-start | bytes 1585160 | tf_op jit(solution)/shard_map/ppermute | solution.py:199
  67.4 30.7 %collective-permute-start.4 = (bf16[344,768]{1,0:T(8,128)(2,1)S(1)}, bf16[344,768]{1,0:T(8,128)(2,1)S(1)}, u32[]{:S(2)}, u32[]{:S(2)}) collective-permute-start(bf16[344,768]{1,0:T(8,128)(2,1)S(1)} %pad_maximum_fusion.16), channel_id=1, source_target_pairs={{0,4},{1,5},{4,0},{5,1},{2,6},{3,7},{6,2},{7,3},{8,12},{9,13},{12,... | collective-permute-start | bytes 1585160 | tf_op jit(solution)/shard_map/ppermute | solution.py:199
  86.4 23.3 %collective-permute-start.5 = (bf16[344,768]{1,0:T(8,128)(2,1)S(1)}, bf16[344,768]{1,0:T(8,128)(2,1)S(1)}, u32[]{:S(2)}, u32[]{:S(2)}) collective-permute-start(bf16[344,768]{1,0:T(8,128)(2,1)S(1)} %pad_maximum_fusion.17), channel_id=1, source_target_pairs={{0,5},{1,4},{4,1},{5,0},{2,7},{3,6},{6,3},{7,2},{8,13},{9,12},{12,... | collective-permute-start | bytes 1585160 | tf_op jit(solution)/shard_map/ppermute | solution.py:199
  90.3 33.2 %collective-permute-start.10 = (bf16[344,768]{1,0:T(8,128)(2,1)S(1)}, bf16[344,768]{1,0:T(8,128)(2,1)S(1)}, u32[]{:S(2)}, u32[]{:S(2)}) collective-permute-start(bf16[344,768]{1,0:T(8,128)(2,1)S(1)} %pad_maximum_fusion.18), channel_id=1, source_target_pairs={{0,1},{1,0},{4,5},{5,4},{2,3},{3,2},{6,7},{7,6},{8,9},{9,8},{12,13... | collective-permute-start | bytes 1585160 | tf_op jit(solution)/shard_map/ppermute | solution.py:199
  91.1 32.5 %collective-permute-start.11 = (bf16[344,768]{1,0:T(8,128)(2,1)S(1)}, bf16[344,768]{1,0:T(8,128)(2,1)S(1)}, u32[]{:S(2)}, u32[]{:S(2)}) collective-permute-start(bf16[344,768]{1,0:T(8,128)(2,1)S(1)} %pad_maximum_fusion.19), channel_id=1, source_target_pairs={{0,4},{1,5},{4,0},{5,1},{2,6},{3,7},{6,2},{7,3},{8,12},{9,13},{12,... | collective-permute-start | bytes 1585160 | tf_op jit(solution)/shard_map/ppermute | solution.py:199
  96.0 36.4 %collective-permute-start.12 = (bf16[344,768]{1,0:T(8,128)(2,1)S(1)}, bf16[344,768]{1,0:T(8,128)(2,1)S(1)}, u32[]{:S(2)}, u32[]{:S(2)}) collective-permute-start(bf16[344,768]{1,0:T(8,128)(2,1)S(1)} %pad_maximum_fusion.20), channel_id=1, source_target_pairs={{0,5},{1,4},{4,1},{5,0},{2,7},{3,6},{6,3},{7,2},{8,13},{9,12},{12,... | collective-permute-start | bytes 1585160 | tf_op jit(solution)/shard_map/ppermute | solution.py:199
  98.0 47.2 %collective-permute-start.16 = (bf16[344,768]{1,0:T(8,128)(2,1)}, bf16[344,768]{1,0:T(8,128)(2,1)S(1)}, u32[]{:S(2)}, u32[]{:S(2)}) collective-permute-start(bf16[344,768]{1,0:T(8,128)(2,1)} %pad_maximum_fusion.21), channel_id=1, source_target_pairs={{0,1},{1,0},{4,5},{5,4},{2,3},{3,2},{6,7},{7,6},{8,9},{9,8},{12,13... | collective-permute-start | bytes 1585160 | tf_op jit(solution)/shard_map/ppermute | solution.py:199
  109.7 35.8 %collective-permute-start.17 = (bf16[344,768]{1,0:T(8,128)(2,1)S(1)}, bf16[344,768]{1,0:T(8,128)(2,1)S(1)}, u32[]{:S(2)}, u32[]{:S(2)}) collective-permute-start(bf16[344,768]{1,0:T(8,128)(2,1)S(1)} %pad_maximum_fusion.22), channel_id=1, source_target_pairs={{0,4},{1,5},{4,0},{5,1},{2,6},{3,7},{6,2},{7,3},{8,12},{9,13},{12,... | collective-permute-start | bytes 1585160 | tf_op jit(solution)/shard_map/ppermute | solution.py:199
  123.5 31.0 %collective-permute-start.18 = (bf16[344,768]{1,0:T(8,128)(2,1)S(1)}, bf16[344,768]{1,0:T(8,128)(2,1)S(1)}, u32[]{:S(2)}, u32[]{:S(2)}) collective-permute-start(bf16[344,768]{1,0:T(8,128)(2,1)S(1)} %pad_maximum_fusion.23), channel_id=1, source_target_pairs={{0,5},{1,4},{4,1},{5,0},{2,7},{3,6},{6,3},{7,2},{8,13},{9,12},{12,... | collective-permute-start | bytes 1585160 | tf_op jit(solution)/shard_map/ppermute | solution.py:199
  123.7 32.9 %collective-permute-start.7 = (bf16[344,256]{1,0:T(8,128)(2,1)}, bf16[344,256]{1,0:T(8,128)(2,1)S(1)}, u32[]{:S(2)}, u32[]{:S(2)}) collective-permute-start(bf16[344,256]{1,0:T(8,128)(2,1)} %get-tuple-element.284), channel_id=1, source_target_pairs={{0,1},{1,0},{4,5},{5,4},{2,3},{3,2},{6,7},{7,6},{8,9},{9,8},{12,13... | collective-permute-start | bytes 528392 | tf_op jit(solution)/shard_map/ppermute | solution.py:199
  132.4 24.2 %collective-permute-start.8 = (bf16[344,256]{1,0:T(8,128)(2,1)S(1)}, bf16[344,256]{1,0:T(8,128)(2,1)S(1)}, u32[]{:S(2)}, u32[]{:S(2)}) collective-permute-start(bf16[344,256]{1,0:T(8,128)(2,1)S(1)} %get-tuple-element.283), channel_id=1, source_target_pairs={{0,4},{1,5},{4,0},{5,1},{2,6},{3,7},{6,2},{7,3},{8,12},{9,13},{12,... | collective-permute-start | bytes 528392 | tf_op jit(solution)/shard_map/ppermute | solution.py:199
  180.3 26.1 %collective-permute-start.22 = (bf16[3,344,1024]{2,1,0:T(8,128)(2,1)}, bf16[3,344,1024]{2,1,0:T(8,128)(2,1)}, u32[]{:S(2)}, u32[]{:S(2)}) collective-permute-start(bf16[3,344,1024]{2,1,0:T(8,128)(2,1)} %param.14), channel_id=1, source_target_pairs={{2,4},{4,2},{3,5},{5,3},{10,12},{12,10},{11,13},{13,11},{18,20},{2... | collective-permute-start | bytes 6340616 | tf_op jit(solution)/shard_map/ppermute | solution.py:193
  286.3 399.0 %reduce-scatter.3.cloned.1.call-start = ((), (), s32[]{:S(2)}) async-start(), calls=%async_computation.6 | async-start | bytes 9437184 | tf_op jit(solution)/shard_map/reduce_scatter | solution.py:392
  313.5 34.8 %collective-permute-start.29 = (bf16[344,256]{1,0:T(8,128)(2,1)S(1)}, bf16[344,256]{1,0:T(8,128)(2,1)S(1)}, u32[]{:S(2)}, u32[]{:S(2)}) collective-permute-start(bf16[344,256]{1,0:T(8,128)(2,1)S(1)} %get-tuple-element.269), channel_id=1, source_target_pairs={{0,1},{1,0},{4,5},{5,4},{2,3},{3,2},{6,7},{7,6},{8,9},{9,8},{12,13... | collective-permute-start | bytes 528392 | tf_op jit(solution)/shard_map/ppermute | solution.py:199
  341.7 21.5 %collective-permute-start.23 = (bf16[344,256]{1,0:T(8,128)(2,1)S(1)}, bf16[344,256]{1,0:T(8,128)(2,1)S(1)}, u32[]{:S(2)}, u32[]{:S(2)}) collective-permute-start(bf16[344,256]{1,0:T(8,128)(2,1)S(1)} %get-tuple-element.273), channel_id=1, source_target_pairs={{0,1},{1,0},{4,5},{5,4},{2,3},{3,2},{6,7},{7,6},{8,9},{9,8},{12,13... | collective-permute-start | bytes 528392 | tf_op jit(solution)/shard_map/ppermute | solution.py:199
  342.9 21.3 %collective-permute-start.24 = (bf16[344,256]{1,0:T(8,128)(2,1)S(1)}, bf16[344,256]{1,0:T(8,128)(2,1)S(1)}, u32[]{:S(2)}, u32[]{:S(2)}) collective-permute-start(bf16[344,256]{1,0:T(8,128)(2,1)S(1)} %get-tuple-element.272), channel_id=1, source_target_pairs={{0,4},{1,5},{4,0},{5,1},{2,6},{3,7},{6,2},{7,3},{8,12},{9,13},{12,... | collective-permute-start | bytes 528392 | tf_op jit(solution)/shard_map/ppermute | solution.py:199
  349.2 29.7 %collective-permute-start.35 = (bf16[344,256]{1,0:T(8,128)(2,1)S(1)}, bf16[344,256]{1,0:T(8,128)(2,1)S(1)}, u32[]{:S(2)}, u32[]{:S(2)}) collective-permute-start(bf16[344,256]{1,0:T(8,128)(2,1)S(1)} %get-tuple-element.265), channel_id=1, source_target_pairs={{0,1},{1,0},{4,5},{5,4},{2,3},{3,2},{6,7},{7,6},{8,9},{9,8},{12,13... | collective-permute-start | bytes 528392 | tf_op jit(solution)/shard_map/ppermute | solution.py:199
  350.3 29.6 %collective-permute-start.36 = (bf16[344,256]{1,0:T(8,128)(2,1)S(1)}, bf16[344,256]{1,0:T(8,128)(2,1)S(1)}, u32[]{:S(2)}, u32[]{:S(2)}) collective-permute-start(bf16[344,256]{1,0:T(8,128)(2,1)S(1)} %get-tuple-element.264), channel_id=1, source_target_pairs={{0,4},{1,5},{4,0},{5,1},{2,6},{3,7},{6,2},{7,3},{8,12},{9,13},{12,... | collective-permute-start | bytes 528392 | tf_op jit(solution)/shard_map/ppermute | solution.py:199
  364.2 43.0 %collective-permute-start.44 = (bf16[344,384]{1,0:T(8,128)(2,1)S(1)}, bf16[344,384]{1,0:T(8,128)(2,1)S(1)}, u32[]{:S(2)}, u32[]{:S(2)}) collective-permute-start(bf16[344,384]{1,0:T(8,128)(2,1)S(1)} %get-tuple-element.240), channel_id=1, source_target_pairs={{0,1},{1,0},{4,5},{5,4},{2,3},{3,2},{6,7},{7,6},{8,9},{9,8},{12,13... | collective-permute-start | bytes 792584 | tf_op jit(solution)/shard_map/ppermute | solution.py:199
  365.2 43.1 %collective-permute-start.45 = (bf16[344,384]{1,0:T(8,128)(2,1)S(1)}, bf16[344,384]{1,0:T(8,128)(2,1)S(1)}, u32[]{:S(2)}, u32[]{:S(2)}) collective-permute-start(bf16[344,384]{1,0:T(8,128)(2,1)S(1)} %get-tuple-element.239), channel_id=1, source_target_pairs={{0,4},{1,5},{4,0},{5,1},{2,6},{3,7},{6,2},{7,3},{8,12},{9,13},{12,... | collective-permute-start | bytes 792584 | tf_op jit(solution)/shard_map/ppermute | solution.py:199
  378.8 30.6 %collective-permute-start.46 = (bf16[344,384]{1,0:T(8,128)(2,1)S(1)}, bf16[344,384]{1,0:T(8,128)(2,1)S(1)}, u32[]{:S(2)}, u32[]{:S(2)}) collective-permute-start(bf16[344,384]{1,0:T(8,128)(2,1)S(1)} %get-tuple-element.238), channel_id=1, source_target_pairs={{0,5},{1,4},{4,1},{5,0},{2,7},{3,6},{6,3},{7,2},{8,13},{9,12},{12,... | collective-permute-start | bytes 792584 | tf_op jit(solution)/shard_map/ppermute | solution.py:199
  379.9 29.5 %collective-permute-start.41 = (bf16[344,384]{1,0:T(8,128)(2,1)S(1)}, bf16[344,384]{1,0:T(8,128)(2,1)S(1)}, u32[]{:S(2)}, u32[]{:S(2)}) collective-permute-start(bf16[344,384]{1,0:T(8,128)(2,1)S(1)} %get-tuple-element.244), channel_id=1, source_target_pairs={{0,1},{1,0},{4,5},{5,4},{2,3},{3,2},{6,7},{7,6},{8,9},{9,8},{12,13... | collective-permute-start | bytes 792584 | tf_op jit(solution)/shard_map/ppermute | solution.py:199
  381.0 29.6 %collective-permute-start.42 = (bf16[344,384]{1,0:T(8,128)(2,1)S(1)}, bf16[344,384]{1,0:T(8,128)(2,1)S(1)}, u32[]{:S(2)}, u32[]{:S(2)}) collective-permute-start(bf16[344,384]{1,0:T(8,128)(2,1)S(1)} %get-tuple-element.243), channel_id=1, source_target_pairs={{0,4},{1,5},{4,0},{5,1},{2,6},{3,7},{6,2},{7,3},{8,12},{9,13},{12,... | collective-permute-start | bytes 792584 | tf_op jit(solution)/shard_map/ppermute | solution.py:199
  410.6 23.0 %collective-permute-start.32 = (bf16[344,384]{1,0:T(8,128)(2,1)S(1)}, bf16[344,384]{1,0:T(8,128)(2,1)S(1)}, u32[]{:S(2)}, u32[]{:S(2)}) collective-permute-start(bf16[344,384]{1,0:T(8,128)(2,1)S(1)} %get-tuple-element.252), channel_id=1, source_target_pairs={{0,1},{1,0},{4,5},{5,4},{2,3},{3,2},{6,7},{7,6},{8,9},{9,8},{12,13... | collective-permute-start | bytes 792584 | tf_op jit(solution)/shard_map/ppermute | solution.py:199
  475.9 27.5 %collective-permute-start.48 = (bf16[344,384]{1,0:T(8,128)(2,1)S(1)}, bf16[344,384]{1,0:T(8,128)(2,1)S(1)}, u32[]{:S(2)}, u32[]{:S(2)}) collective-permute-start(bf16[344,384]{1,0:T(8,128)(2,1)S(1)} %get-tuple-element.236), channel_id=1, source_target_pairs={{0,1},{1,0},{4,5},{5,4},{2,3},{3,2},{6,7},{7,6},{8,9},{9,8},{12,13... | collective-permute-start | bytes 792584 | tf_op jit(solution)/shard_map/ppermute | solution.py:199
  477.0 26.5 %collective-permute-start.49 = (bf16[344,384]{1,0:T(8,128)(2,1)S(1)}, bf16[344,384]{1,0:T(8,128)(2,1)S(1)}, u32[]{:S(2)}, u32[]{:S(2)}) collective-permute-start(bf16[344,384]{1,0:T(8,128)(2,1)S(1)} %get-tuple-element.235), channel_id=1, source_target_pairs={{0,4},{1,5},{4,0},{5,1},{2,6},{3,7},{6,2},{7,3},{8,12},{9,13},{12,... | collective-permute-start | bytes 792584 | tf_op jit(solution)/shard_map/ppermute | solution.py:199
  477.1 26.5 %collective-permute-start.50 = (bf16[344,384]{1,0:T(8,128)(2,1)S(1)}, bf16[344,384]{1,0:T(8,128)(2,1)S(1)}, u32[]{:S(2)}, u32[]{:S(2)}) collective-permute-start(bf16[344,384]{1,0:T(8,128)(2,1)S(1)} %get-tuple-element.234), channel_id=1, source_target_pairs={{0,5},{1,4},{4,1},{5,0},{2,7},{3,6},{6,3},{7,2},{8,13},{9,12},{12,... | collective-permute-start | bytes 792584 | tf_op jit(solution)/shard_map/ppermute | solution.py:199
  479.9 128.6 %collective-permute-start.54 = (bf16[512,2560]{1,0:T(8,128)(2,1)}, bf16[512,2560]{1,0:T(8,128)(2,1)}, u32[]{:S(2)}, u32[]{:S(2)}) collective-permute-start(bf16[512,2560]{1,0:T(8,128)(2,1)} %pad_maximum_fusion), channel_id=1, source_target_pairs={{0,4},{4,0},{1,5},{5,1},{2,6},{6,2},{3,7},{7,3},{8,12},{12,8},{9,1... | collective-permute-start | bytes 7864328 | tf_op jit(solution)/shard_map/ppermute | solution.py:199
  521.4 82.3 %collective-permute-start.60 = (bf16[512,1536]{1,0:T(8,128)(2,1)}, bf16[512,1536]{1,0:T(8,128)(2,1)}, u32[]{:S(2)}, u32[]{:S(2)}) collective-permute-start(bf16[512,1536]{1,0:T(8,128)(2,1)} %convolution_convert_fusion.3), channel_id=1, source_target_pairs={{0,4},{4,0},{1,5},{5,1},{2,6},{6,2},{3,7},{7,3},{8,12},{12,8},{9,1... | collective-permute-start | bytes 4718600 | tf_op jit(solution)/shard_map/ppermute | solution.py:199
  531.1 122.5 %collective-permute-start.47 = (bf16[3,344,1024]{2,1,0:T(8,128)(2,1)}, bf16[3,344,1024]{2,1,0:T(8,128)(2,1)S(1)}, u32[]{:S(2)}, u32[]{:S(2)}) collective-permute-start(bf16[3,344,1024]{2,1,0:T(8,128)(2,1)} %bitcast.153), channel_id=1, source_target_pairs={{2,4},{4,2},{3,5},{5,3},{10,12},{12,10},{11,13},{13,11},{18,20},{2... | collective-permute-start | bytes 6340616 | tf_op jit(solution)/shard_map/ppermute | solution.py:193
  531.9 89.2 %collective-permute-start.51 = (bf16[344,1024]{1,0:T(8,128)(2,1)}, bf16[344,1024]{1,0:T(8,128)(2,1)S(1)}, u32[]{:S(2)}, u32[]{:S(2)}) collective-permute-start(bf16[344,1024]{1,0:T(8,128)(2,1)} %get-tuple-element.182), channel_id=1, source_target_pairs={{2,4},{4,2},{3,5},{5,3},{10,12},{12,10},{11,13},{13,11},{18,20},{2... | collective-permute-start | bytes 2113544 | tf_op jit(solution)/shard_map/ppermute | solution.py:193
  538.1 63.7 %collective-permute-start.76 = (f32[14,1024]{1,0:T(8,128)S(1)}, f32[14,1024]{1,0:T(8,128)S(1)}, u32[]{:S(2)}, u32[]{:S(2)}) collective-permute-start(f32[14,1024]{1,0:T(8,128)S(1)} %add.622), channel_id=1, source_target_pairs={{0,2},{2,0},{1,3},{3,1},{4,6},{6,4},{5,7},{7,5},{8,10},{10,8},{9,1... | collective-permute-start | bytes 172040 | tf_op jit(solution)/shard_map/ppermute | solution.py:199
  601.8 20.9 %collective-permute-start.52 = (bf16[344,1024]{1,0:T(8,128)(2,1)S(1)}, bf16[344,1024]{1,0:T(8,128)(2,1)S(1)}, u32[]{:S(2)}, u32[]{:S(2)}) collective-permute-start(bf16[344,1024]{1,0:T(8,128)(2,1)S(1)} %fusion.52), channel_id=1, source_target_pairs={{2,4},{4,2},{3,5},{5,3},{10,12},{12,10},{11,13},{13,11},{18,20},{2... | collective-permute-start | bytes 2113544 | tf_op jit(solution)/shard_map/ppermute | solution.py:193
  603.7 40.5 %collective-permute-start.53 = (bf16[344,1024]{1,0:T(8,128)(2,1)S(1)}, bf16[344,1024]{1,0:T(8,128)(2,1)S(1)}, u32[]{:S(2)}, u32[]{:S(2)}) collective-permute-start(bf16[344,1024]{1,0:T(8,128)(2,1)S(1)} %copy-done.73), channel_id=1, source_target_pairs={{2,4},{4,2},{3,5},{5,3},{10,12},{12,10},{11,13},{13,11},{18,20},{2... | collective-permute-start | bytes 2113544 | tf_op jit(solution)/shard_map/ppermute | solution.py:193
  620.6 21.8 %collective-permute-start.55 = (bf16[2,128,2560]{2,1,0:T(8,128)(2,1)S(1)}, bf16[2,128,2560]{2,1,0:T(8,128)(2,1)S(1)}, u32[]{:S(2)}, u32[]{:S(2)}) collective-permute-start(bf16[2,128,2560]{2,1,0:T(8,128)(2,1)S(1)} %bitcast.155), channel_id=1, source_target_pairs={{0,8},{4,20},{8,0},{12,28},{16,24},{20,4},{24,16},{28,12},{1,9},{5... | collective-permute-start | bytes 3932168 | tf_op jit(solution)/shard_map/ppermute | solution.py:259
  683.4 20.0 %collective-permute-start.69 = (bf16[256,1024]{1,0:T(8,128)(2,1)}, bf16[256,1024]{1,0:T(8,128)(2,1)}, u32[]{:S(2)}, u32[]{:S(2)}) collective-permute-start(bf16[256,1024]{1,0:T(8,128)(2,1)} %constant_dynamic-slice_fusion.2), channel_id=1, source_target_pairs={{0,1},{1,0},{2,3},{3,2},{4,5},{5,4},{6,7},{7,6},{8,9},{9,8},{10,11... | collective-permute-start | bytes 1572872 | tf_op jit(solution)/shard_map/ppermute | solution.py:199
  686.5 33.2 %collective-permute-start.66 = (bf16[64,4096]{1,0:T(8,128)(2,1)S(1)}, bf16[64,4096]{1,0:T(8,128)(2,1)S(1)}, u32[]{:S(2)}, u32[]{:S(2)}) collective-permute-start(bf16[64,4096]{1,0:T(8,128)(2,1)S(1)} %constant_dynamic-slice_fusion.3), channel_id=1, source_target_pairs={{0,1},{1,0},{2,3},{3,2},{4,5},{5,4},{6,7},{7,6},{8,9},{9,8},{10,11... | collective-permute-start | bytes 1572872 | tf_op jit(solution)/shard_map/ppermute | solution.py:199
  704.6 36.9 %collective-permute-start.70 = (bf16[256,1024]{1,0:T(8,128)(2,1)S(1)}, bf16[256,1024]{1,0:T(8,128)(2,1)S(1)}, u32[]{:S(2)}, u32[]{:S(2)}) collective-permute-start(bf16[256,1024]{1,0:T(8,128)(2,1)S(1)} %dynamic-slice_add_fusion), channel_id=1, source_target_pairs={{0,2},{2,0},{1,3},{3,1},{4,6},{6,4},{5,7},{7,5},{8,10},{10,8},{9,1... | collective-permute-start | bytes 1572872 | tf_op jit(solution)/shard_map/ppermute | solution.py:199
  720.7 28.5 %collective-permute-start.67 = (bf16[64,4096]{1,0:T(8,128)(2,1)}, bf16[64,4096]{1,0:T(8,128)(2,1)}, u32[]{:S(2)}, u32[]{:S(2)}) collective-permute-start(bf16[64,4096]{1,0:T(8,128)(2,1)} %dynamic-slice_add_fusion.1), channel_id=1, source_target_pairs={{0,2},{2,0},{1,3},{3,1},{4,6},{6,4},{5,7},{7,5},{8,10},{10,8},{9,1... | collective-permute-start | bytes 1572872 | tf_op jit(solution)/shard_map/ppermute | solution.py:199
  (180 other events, 2258.9 us)
Sparse Core Ops, SparseCore 0:
  10.5 49.3 all-gather.6
  61.8 27.8 all-gather.8
  91.6 54.3 all-gather.10
  147.8 54.3 all-gather.12
  286.4 98.6 reduce-scatter.4
  435.5 73.2 reduce-scatter.2
